TPU v7x, 256 devices: a whole 4x4x8 slice. The times are simulated.
256 devices in a mesh: srow: 16 (over x, y_hi, core), scol: 16 (over z, y_lo).
Axes of the slice: x: 4, y: 4 (y_hi: 2, y_lo: 2; y = y_hi * 2 + y_lo), z: 8, core: 2. Of those that a mesh axis runs over, the one named last changes fastest.
Arguments:
- patterns: float32 [64, 64, 128, 128], P('srow', 'scol'), may hold values from 0.01 to 800, as said below
- offsets: int32 [64, 64, 2], P('srow', 'scol'), may hold values from 0 to 71, as said below
- object_field: float32 [2, 1152, 1152], P(None, 'srow', 'scol'), may hold values from -5 to 5
- probe: float32 [2, 2, 128, 128], replicated, may hold values from -6 to 6
Outputs:
- new_object: float32 [2, 1152, 1152], P(None, 'srow', 'scol')
- new_probe: float32 [2, 2, 128, 128], replicated
Inputs may be any that keep to these rules, and one draw needn't show every extreme that they name: `patterns`: patterns are positive. `offsets`: position (r, c) has its centre at tile row 16 * (r mod 4) plus 0 to 23, and tile column 16 * (c mod 4) plus 0 to 23.
All inputs are finite; a program needn't handle non-finite values.
Results may differ from a plain program's by a relative error of at most 0.0003.
Values sent between devices are 32-bit elements; how exact they have to be, the bound alone decides.
No kernel may reach another device: no remote copies, remote signals or barrier semaphores. Data moves between devices by JAX's collectives and lax.ppermute only.
A program may use at most 64 MiB of HBM per device.

v0:
```python
import math

import jax
import jax.numpy as jnp
from jax import lax
from jax.sharding import PartitionSpec as P

W = 128
PR = 4
PC = 4


obj_rate = 0.2
probe_rate = 0.5
amp_floor = 0.1
highest = lax.Precision.HIGHEST


def extended_2(cells, sides, width):
    for axis, dim in sides:
        count = lax.axis_size(axis)
        head = lax.slice_in_dim(cells, 0, width, axis=dim)
        tail = lax.slice_in_dim(cells, cells.shape[dim] - width, cells.shape[dim], axis=dim)
        cells = jnp.concatenate(
            [
                lax.ppermute(tail, axis, [(i, (i + 1) % count) for i in range(count)]),
                cells,
                lax.ppermute(head, axis, [((i + 1) % count, i) for i in range(count)]),
            ],
            axis=dim,
        )
    return cells


def signed_freq(length):
    counter = jnp.arange(length, dtype=jnp.int32)
    return ((counter + length // 2) % length - length // 2).astype(jnp.float32)


def dft_tables(length):
    counter = jnp.arange(length, dtype=jnp.int32)
    product = counter[:, None] * counter[None, :] % length
    angles = 2.0 * math.pi / length * product.astype(jnp.float32)
    return (jnp.cos(angles), jnp.sin(angles))


def rows_by(matrix, values):
    return jnp.einsum("uk,...kv->...uv", matrix, values, precision=highest)


def cols_by(values, matrix):
    return jnp.einsum("...uk,kv->...uv", values, matrix, precision=highest)


def transform(real_part, imag_part, cos_table, sin_table, turn_sign, real_only=False):
    length = cos_table.shape[0]
    if imag_part is None:
        first_re = rows_by(cos_table, real_part)
        first_im = turn_sign * rows_by(sin_table, real_part)
    else:
        first_re = rows_by(cos_table, real_part) - turn_sign * rows_by(sin_table, imag_part)
        first_im = rows_by(cos_table, imag_part) + turn_sign * rows_by(sin_table, real_part)
    second_re = (cols_by(first_re, cos_table) - turn_sign * cols_by(first_im, sin_table)) / length
    if real_only:
        return second_re
    second_im = (cols_by(first_im, cos_table) + turn_sign * cols_by(first_re, sin_table)) / length
    return (second_re, second_im)


def fold_rims(values, axis_dim, tile_len, half_width):
    full_len = values.shape[axis_dim]
    interior = lax.slice_in_dim(values, 2 * half_width, 2 * half_width + tile_len, axis=axis_dim)
    low_rim = lax.slice_in_dim(values, 0, half_width, axis=axis_dim)
    high_rim = lax.slice_in_dim(values, full_len - half_width, full_len, axis=axis_dim)
    low_pad = [
        (0, tile_len - half_width) if place == axis_dim else (0, 0) for place in range(values.ndim)
    ]
    high_pad = [
        (tile_len - half_width, 0) if place == axis_dim else (0, 0) for place in range(values.ndim)
    ]
    return interior + jnp.pad(low_rim, low_pad) + jnp.pad(high_rim, high_pad)


def on_device(patterns, offsets, object_field, probe):
    row_dev = lax.axis_size("srow")
    col_dev = lax.axis_size("scol")
    half_width = W // 2
    cos_table, sin_table = dft_tables(W)
    frequency = signed_freq(W)
    weights = jnp.sum(patterns, axis=(2, 3))
    com_row = jnp.einsum("abij,i->ab", patterns, frequency, precision=highest) / weights
    com_col = jnp.einsum("abij,j->ab", patterns, frequency, precision=highest) / weights
    centres = jnp.stack([com_row, com_col])
    row_pos = (
        (lax.axis_index("srow") * PR + jnp.arange(PR, dtype=jnp.int32)).astype(jnp.float32) + 0.5
    ) / (PR * row_dev) - 0.5
    col_pos = (
        (lax.axis_index("scol") * PC + jnp.arange(PC, dtype=jnp.int32)).astype(jnp.float32) + 0.5
    ) / (PC * col_dev) - 0.5
    row_grid = jnp.broadcast_to(row_pos[:, None], (PR, PC))
    col_grid = jnp.broadcast_to(col_pos[None, :], (PR, PC))
    first_sums = jnp.stack(
        [jnp.sum(weights), jnp.sum(weights * row_grid), jnp.sum(weights * col_grid)]
    )
    centre_moment = jnp.einsum("kab,ab->k", centres, weights, precision=highest)
    first_sums, centre_moment = lax.psum((first_sums, centre_moment), ("srow", "scol"))
    mean_row = first_sums[1] / first_sums[0]
    mean_col = first_sums[2] / first_sums[0]
    mean_centre = centre_moment / first_sums[0]
    spread = jnp.stack([row_grid - mean_row, col_grid - mean_col])
    deviation = centres - mean_centre[:, None, None]
    second_mom = jnp.einsum("iab,jab,ab->ij", spread, spread, weights, precision=highest)
    cross_mom = jnp.einsum("iab,kab,ab->ik", spread, deviation, weights, precision=highest)
    second_mom, cross_mom = lax.psum((second_mom, cross_mom), ("srow", "scol"))
    determ = second_mom[0, 0] * second_mom[1, 1] - second_mom[0, 1] * second_mom[1, 0]
    inverse = (
        jnp.stack(
            [
                jnp.stack([second_mom[1, 1], -second_mom[0, 1]]),
                jnp.stack([-second_mom[1, 0], second_mom[0, 0]]),
            ]
        )
        / determ
    )
    slopes = jnp.dot(inverse, cross_mom, precision=highest)
    descan = mean_centre[:, None, None] + jnp.einsum(
        "iab,ik->kab", spread, slopes, precision=highest
    )
    extended = extended_2(object_field, (("srow", 1), ("scol", 2)), half_width)
    pattern_flat = patterns.reshape(-1, W, W)
    spec_re, spec_im = transform(pattern_flat, None, cos_table, sin_table, -1.0)
    shift_r = descan[0].reshape(-1)
    shift_c = descan[1].reshape(-1)
    phases = (
        2.0
        * math.pi
        / W
        * (
            shift_r[:, None, None] * frequency[None, :, None]
            + shift_c[:, None, None] * frequency[None, None, :]
        )
    )
    turn_cos = jnp.cos(phases)
    turn_sin = jnp.sin(phases)
    rot_re = spec_re * turn_cos - spec_im * turn_sin
    rot_im = spec_re * turn_sin + spec_im * turn_cos
    shifted = transform(rot_re, rot_im, cos_table, sin_table, 1.0, real_only=True)
    targets = jnp.sqrt(jnp.maximum(shifted, 0.0))
    row_start = offsets[:, :, 0].reshape(-1)
    col_start = offsets[:, :, 1].reshape(-1)
    position_count = row_start.shape[0]

    def cut_one(place, gathered):
        corner = (jnp.int32(0), row_start[place], col_start[place])
        piece = lax.dynamic_slice(extended, corner, (2, W, W))
        return lax.dynamic_update_slice(
            gathered, piece[None], (place, jnp.int32(0), jnp.int32(0), jnp.int32(0))
        )

    windows = lax.fori_loop(
        0, position_count, cut_one, jnp.zeros((position_count, 2, W, W), jnp.float32)
    )
    win_re = windows[:, 0][:, None]
    win_im = windows[:, 1][:, None]
    probe_re = probe[:, 0][None]
    probe_im = probe[:, 1][None]
    exit_re = probe_re * win_re - probe_im * win_im
    exit_im = probe_re * win_im + probe_im * win_re
    far_re, far_im = transform(exit_re, exit_im, cos_table, sin_table, -1.0)
    amplitude = jnp.sqrt(jnp.sum(far_re * far_re + far_im * far_im, axis=1))
    factor = (1.0 - targets / jnp.maximum(amplitude, amp_floor))[:, None]
    back_re, back_im = transform(far_re * factor, far_im * factor, cos_table, sin_table, 1.0)
    grad_re = jnp.sum(probe_re * back_re + probe_im * back_im, axis=1)
    grad_im = jnp.sum(probe_re * back_im - probe_im * back_re, axis=1)
    probe_grad = jnp.stack(
        [
            jnp.sum(win_re * back_re + win_im * back_im, axis=0),
            jnp.sum(win_re * back_im - win_im * back_re, axis=0),
        ],
        axis=1,
    )
    grad_stack = jnp.stack([grad_re, grad_im], axis=1)

    def add_one(place, accum):
        corner = (jnp.int32(0), row_start[place], col_start[place])
        current = lax.dynamic_slice(accum, corner, (2, W, W))
        return lax.dynamic_update_slice(accum, current + grad_stack[place], corner)

    ext_grad = lax.fori_loop(0, position_count, add_one, jnp.zeros(extended.shape, jnp.float32))
    tile_rows = object_field.shape[1]
    tile_cols = object_field.shape[2]
    padded = extended_2(ext_grad, (("srow", 1), ("scol", 2)), half_width)
    grad_tile = fold_rims(fold_rims(padded, 1, tile_rows, half_width), 2, tile_cols, half_width)
    probe_power = jnp.max(jnp.sum(probe * probe, axis=(0, 1)))
    new_object = object_field - obj_rate * grad_tile / probe_power
    positions_all = PR * row_dev * PC * col_dev
    summed = lax.psum(probe_grad, ("srow", "scol"))
    new_probe = probe - probe_rate * summed / positions_all
    return (new_object, new_probe)


def solution(mesh):
    placed = (P("srow", "scol", None, None), P("srow", "scol", None), P(None, "srow", "scol"), P())
    return jax.shard_map(
        on_device,
        mesh=mesh,
        in_specs=placed,
        out_specs=(P(None, "srow", "scol"), P()),
        check_vma=False,
    )
```

profile of v0, /device:TPU:1, one launch (start us, length us, event | category | flops | bytes accessed | tf_op | source)
XLA Modules:
  0.0 756.2 jit_solution(8100221730847094329)
XLA Ops:
  14.1 4.3 collective-permute-start
  18.5 78.5 %all-reduce.3 = (f32[3]{0:T(128)S(1)}, f32[2]{0:T(128)S(1)}) all-reduce(f32[3]{0:T(128)S(1)} %pad_maximum_fusion.10, f32[2]{0:T(128)S(1)} %convolution_bitcast_fusion.4), channel_id=1, replica_groups=mesh['srow'=16,'scol'=16] {'srow','scol'}, use_global_device_ids=true, to_apply=%region_9.10 | all-reduce | flops 5 | bytes 40 | tf_op jit(solution)/shard_map/psum | solution.py:106
  102.2 73.5 %all-reduce.2 = (f32[2,2]{1,0:T(2,128)S(1)}, f32[2,2]{1,0:T(2,128)S(1)}) all-reduce(f32[2,2]{1,0:T(2,128)S(1)} %convolution_bitcast_fusion.2, f32[2,2]{1,0:T(2,128)S(1)} %convolution_bitcast_fusion.3), channel_id=1, replica_groups=mesh['srow'=16,'scol'=16] {'srow','scol'}, use_global_device_ids=true, to_apply=%region_11.12 | all-reduce | flops 8 | bytes 64 | tf_op jit(solution)/shard_map/psum | solution.py:114
  189.6 6.0 fusion.95
  195.6 5.8 fusion.99
  201.4 7.0 fusion.45
  208.5 5.8 fusion.46
  222.2 4.1 collective-permute-done.2
  226.3 4.3 collective-permute-done.3
  231.8 80.8 %while.26 = (s32[]{:T(128)}, f32[16,2,128,128]{3,2,0,1:T(8,128)S(1)}, s32[16]{0:T(128)S(1)}, s32[16]{0:T(128)S(1)}, f32[2,200,200]{2,1,0:T(8,128)S(1)}, /*index=5*/s32[]{:T(128)}, s32[]{:T(128)}, s32[]{:T(128)}) while((s32[]{:T(128)}, f32[16,2,128,128]{3,2,0,1:T(8,128)S(1)}, s32[16]{0:T(128)S(1)}, s32[16]{0:T(128)S(1)}, ...), condition=%wide.region_1.2_spmd, body=%wide.region_0.1_spmd.sunk | while | flops 8 | bytes 262333 | solution.py:160
  326.4 3.7 fusion.8
  332.4 3.6 multiply_subtract_fusion
  335.9 3.9 add_reduce_fusion.2
  342.2 3.6 fusion.22
  345.8 3.6 fusion.20
  349.4 4.1 fusion.31
  353.5 3.7 fusion.2
  357.2 3.7 fusion
  361.1 3.8 fusion.28
  364.9 3.6 fusion.38
  368.5 5.0 add_reduce_fusion
  373.7 119.0 %while.27 = (s32[]{:T(128)}, f32[2,200,200]{2,1,0:T(8,128)S(1)}, s32[16]{0:T(128)S(1)}, s32[16]{0:T(128)S(1)}, f32[16,2,128,128]{3,2,1,0:T(8,128)S(1)}, /*index=5*/s32[]{:T(128)}, s32[]{:T(128)}, s32[]{:T(128)}) while((s32[]{:T(128)}, f32[2,200,200]{2,1,0:T(8,128)S(1)}, s32[16]{0:T(128)S(1)}, s32[16]{0:T(128)S(1)}, ...), condition=%wide.region_16.17_spmd, body=%wide.region_15.16_spmd.sunk | while | flops 32776 | bytes 655553 | solution.py:189
  497.9 4.7 collective-permute-done.5
  506.5 238.5 %all-reduce.6.cloned.1.call-done = f32[2,2,128,128]{3,2,1,0:T(8,128)} async-done(((f32[2,2,128,128]{3,2,1,0:T(8,128)}), f32[2,2,128,128]{3,2,1,0:T(8,128)}) %all-reduce.6.cloned.1.call-update) | async-done | bytes 262160 | tf_op jit(solution)/shard_map/psum | solution.py:197
  (219 shorter events, 138.5 us)
Async XLA Ops:
  7.2 171.6 %copy-start = (f32[4,4,128,128]{3,2,1,0:T(8,128)S(1)}, f32[4,4,128,128]{3,2,1,0:T(8,128)}, u32[]{:S(2)}) copy-start(f32[4,4,128,128]{3,2,1,0:T(8,128)} %param.8) | copy-start | bytes 3145732
  7.2 737.8 %all-reduce.6.cloned.1.call-start = ((), (), s32[]{:S(2)}) async-start(), calls=%async_computation | async-start | bytes 524288 | tf_op jit(solution)/shard_map/psum | solution.py:197
  14.1 203.8 %collective-permute-start = (f32[2,64,72]{2,1,0:T(8,128)S(1)}, f32[2,64,72]{2,1,0:T(8,128)S(1)}, u32[]{:S(2)}, u32[]{:S(2)}) collective-permute-start(f32[2,64,72]{2,1,0:T(8,128)S(1)} %get-tuple-element.249), channel_id=1, source_target_pairs={{0,16},{16,32},{32,48},{48,64},{64,80},{80,96},{96,112},{112,128},... | collective-permute-start | bytes 110600 | tf_op jit(solution)/shard_map/ppermute | solution.py:26
  101.5 116.5 %collective-permute-start.1 = (f32[2,64,72]{2,1,0:T(8,128)S(1)}, f32[2,64,72]{2,1,0:T(8,128)S(1)}, u32[]{:S(2)}, u32[]{:S(2)}) collective-permute-start(f32[2,64,72]{2,1,0:T(8,128)S(1)} %get-tuple-element.248), channel_id=1, source_target_pairs={{16,0},{32,16},{48,32},{64,48},{80,64},{96,80},{112,96},{128,112},... | collective-permute-start | bytes 110600 | tf_op jit(solution)/shard_map/ppermute | solution.py:28
  214.3 3.0 copy-start.3
  214.3 3.7 copy-start.5
  214.3 7.5 copy-start.10
  218.2 8.2 %collective-permute-start.2 = (f32[2,200,64]{2,1,0:T(8,128)S(1)}, f32[2,200,64]{2,1,0:T(8,128)S(1)}, u32[]{:S(2)}, u32[]{:S(2)}) collective-permute-start(f32[2,200,64]{2,1,0:T(8,128)S(1)} %get-tuple-element.246), channel_id=1, source_target_pairs={{0,1},{1,2},{2,3},{3,4},{4,5},{5,6},{6,7},{7,8},{8,9},{9,10},{10,1... | collective-permute-start | bytes 307208 | tf_op jit(solution)/shard_map/ppermute | solution.py:26
  219.3 11.3 %collective-permute-start.3 = (f32[2,200,64]{2,1,0:T(8,128)S(1)}, f32[2,200,64]{2,1,0:T(8,128)}, u32[]{:S(2)}, u32[]{:S(2)}) collective-permute-start(f32[2,200,64]{2,1,0:T(8,128)S(1)} %get-tuple-element.247), channel_id=1, source_target_pairs={{1,0},{2,1},{3,2},{4,3},{5,4},{6,5},{7,6},{8,7},{9,8},{10,9},{11,1... | collective-permute-start | bytes 307208 | tf_op jit(solution)/shard_map/ppermute | solution.py:28
  312.6 1.7 copy-start.1
  335.9 3.9 copy-start.6
  335.9 3.9 copy-start.7
  357.2 3.7 copy-start.2
  364.9 3.6 copy-start.8
  364.9 3.6 copy-start.9
  492.8 252.2 %copy-start.4 = (f32[2,2,128,128]{3,2,1,0:T(8,128)S(1)}, f32[2,2,128,128]{3,2,1,0:T(8,128)}, u32[]{:S(2)}) copy-start(f32[2,2,128,128]{3,2,1,0:T(8,128)} %param.11) | copy-start | bytes 786436
  492.8 5.1 collective-permute-start.4
  495.9 251.4 %copy-start.11 = (pred[72]{0:T(512)(128)(4,1)S(1)}, pred[72]{0:T(512)(128)(4,1)}, u32[]{:S(2)}) copy-start(pred[72]{0:T(512)(128)(4,1)} %constant.140.clone.1) | copy-start | bytes 220
  496.7 6.0 collective-permute-start.5
  502.8 244.5 %collective-permute-start.6 = (f32[2,328,64]{2,1,0:T(8,128)S(1)}, f32[2,328,64]{2,1,0:T(8,128)S(1)}, u32[]{:S(2)}, u32[]{:S(2)}) collective-permute-start(f32[2,328,64]{2,1,0:T(8,128)S(1)} %get-tuple-element.236), channel_id=1, source_target_pairs={{0,1},{1,2},{2,3},{3,4},{4,5},{5,6},{6,7},{7,8},{8,9},{9,10},{10,1... | collective-permute-start | bytes 503816 | tf_op jit(solution)/shard_map/ppermute | solution.py:26
  502.9 244.4 %collective-permute-start.7 = (f32[2,328,64]{2,1,0:T(8,128)S(1)}, f32[2,328,64]{2,1,0:T(8,128)S(1)}, u32[]{:S(2)}, u32[]{:S(2)}) collective-permute-start(f32[2,328,64]{2,1,0:T(8,128)S(1)} %get-tuple-element.237), channel_id=1, source_target_pairs={{1,0},{2,1},{3,2},{4,3},{5,4},{6,5},{7,6},{8,7},{9,8},{10,9},{11,1... | collective-permute-start | bytes 503816 | tf_op jit(solution)/shard_map/ppermute | solution.py:28
Sparse Core Ops, SparseCore 0:
  496.8 248.0 all-reduce.5
where the time goes:
time: 762 us; the launch traced here: 756 us
  waiting for transfers between devices  253 us (33%)
  blocking collectives  152 us (20%)
  loops' own time  122 us (16%)
  matrix products  93.4 us (12%)
  local copies, waits for them, and re-layouts  83.1 us (11%)
  between operations  21.2 us (3%)
  other arithmetic  16.3 us (2%)
  starting transfers between devices  15.6 us (2%)
    psum x1, waiting for transfers between devices, on_device(): summed = lax.psum(probe_grad, ('srow', 'scol'))  238 us
    psum x1, blocking collectives, on_device(): lax.psum((first_sums, centre_moment), ('srow', 'scol'))  78.5 us
    psum x1, blocking collectives, on_device(): second_mom, cross_mom = lax.psum((second_mom, cross_mom), ('srow', 'scol'))  73.5 us
    another operation x1, loops' own time, on_device(): lax.fori_loop(0, position_count, add_one, jnp.zeros(extended.shape, jnp.f...  62.7 us
    another operation x1, loops' own time, on_device(): lax.fori_loop(0, position_count, cut_one, jnp.zeros((position_count, 2, W...  59.2 us
    dot_general x14, matrix products, rows_by(): return jnp.einsum('uk,...kv->...uv', matrix, values, precision=highest)  51.1 us
    dot_general x14, matrix products, cols_by(): return jnp.einsum('...uk,kv->...uv', values, matrix, precision=highest)  40.9 us
    dynamic_update_slice x16, local copies, waits for them, and re-layouts, add_one(): return lax.dynamic_update_slice(accum, current + grad_stack[place], corner)  35.7 us
  transfers between devices with their start and end apart: 9, of which 5 were waited for; matrix products, arithmetic and copies ran while one was open for 6% of the time, Pallas kernels for 0%

commit v1 on v0

v1 whole, which is shorter than its diff:
```python
import math

import jax
import jax.numpy as jnp
import ml_dtypes
import numpy as np
from jax import lax
from jax.experimental import pallas as pl
from jax.experimental.pallas import tpu as pltpu
from jax.sharding import PartitionSpec as P

W = 128
HALF = W // 2
MODES = 2
PR = 4
PC = 4
POSITIONS = PR * PC
TILE = 72
EXT = TILE + W

obj_rate = 0.2
probe_rate = 0.5
amp_floor = 0.1
highest = lax.Precision.HIGHEST
f32 = jnp.float32
bf16 = jnp.bfloat16


def dft_tables():
    counter = np.arange(W)
    angles = 2.0 * np.pi / W * (counter[:, None] * counter[None, :] % W)
    cos, sin = np.cos(angles), np.sin(angles)
    pair = np.block([[cos, -sin], [sin, cos]])

    def parts(matrix, axis):
        high = matrix.astype(ml_dtypes.bfloat16)
        low = (matrix - high.astype(np.float64)).astype(ml_dtypes.bfloat16)
        return np.concatenate([high, high, low], axis=axis)

    right_fwd = parts(pair / 16, 0)
    left_fwd = parts(pair.T / 8, 1)
    right_inv = parts(pair.T / 16, 0)
    left_inv = parts(pair / 8, 1)
    return right_fwd, left_fwd, right_inv, left_inv


def shift_tables():
    counter = np.arange(W)
    freq = np.where(counter <= HALF, counter, counter - HALF)
    angles = 2.0 * np.pi / W * (freq[:, None] * counter[None, :] % W)
    weight = np.where((counter == 0) | (counter == HALF), 1.0, 2.0)[:, None] / W
    is_cos = (counter <= HALF)[:, None]
    cols = np.where(is_cos, np.cos(angles), np.sin(angles)) * weight
    rows = np.where(is_cos, np.cos(angles), -np.sin(angles)) * weight
    return np.stack([cols, rows]).astype(np.float32)


def split(values):
    high = values.astype(bf16)
    low = (values - high.astype(f32)).astype(bf16)
    return high, low


def right_by(values, table):
    high, low = split(values)
    return jnp.dot(jnp.concatenate([high, low, high], axis=1), table, preferred_element_type=f32)


def left_by(table, values):
    high, low = split(values)
    return jnp.dot(table, jnp.concatenate([high, low, high], axis=0), preferred_element_type=f32)


def swap_blocks(values):
    top = jnp.concatenate([values[:W, :W], values[W:, :W]], axis=1)
    bottom = jnp.concatenate([values[:W, W:], values[W:, W:]], axis=1)
    return jnp.concatenate([top, bottom], axis=0)


def lane_iota(shape):
    return lax.broadcasted_iota(jnp.int32, shape, len(shape) - 1)


def row_iota(shape):
    return lax.broadcasted_iota(jnp.int32, shape, len(shape) - 2)


def place_of(place_ref, row_dev, col_dev, shape):
    position = row_iota(shape)
    row = (place_ref[0] * PR + position // PC).astype(f32)
    col = (place_ref[1] * PC + position % PC).astype(f32)
    return (row + 0.5) / (PR * row_dev) - 0.5, (col + 0.5) / (PC * col_dev) - 0.5


def sums_kernel(row_dev, col_dev, place_ref, patterns_ref, out_ref, total_ref, tilt_ref):
    k = row_iota((W, W))
    freq = (((k + HALF) % W) - HALF).astype(f32)
    for p in range(POSITIONS):
        pattern = patterns_ref[p]
        total_ref[p : p + 1, :] = jnp.sum(pattern, axis=0, keepdims=True)
        tilt_ref[p : p + 1, :] = jnp.sum(pattern * freq, axis=0, keepdims=True)
    lane = lane_iota((POSITIONS, W))
    col_freq = (((lane + HALF) % W) - HALF).astype(f32)
    total = total_ref[...]
    weight = jnp.sum(total, axis=1, keepdims=True)
    tilt_row = jnp.sum(tilt_ref[...], axis=1, keepdims=True)
    tilt_col = jnp.sum(total * col_freq, axis=1, keepdims=True)
    row, col = place_of(place_ref, row_dev, col_dev, (POSITIONS, W))
    terms = [
        weight,
        weight * row,
        weight * col,
        weight * row * row,
        weight * row * col,
        weight * col * col,
        tilt_row,
        tilt_row * row,
        tilt_row * col,
        tilt_col,
        tilt_col * row,
        tilt_col * col,
    ]
    packed = jnp.zeros((POSITIONS, W), f32)
    for i, term in enumerate(terms):
        packed = jnp.where(lane == i, term, packed)
    summed = jnp.sum(packed, axis=0, keepdims=True)
    out_ref[...] = jnp.broadcast_to(summed, out_ref.shape)


def cut_window(ext_ref, part, row, col):
    lane = lane_iota((W, W))
    shift = lax.rem(W - col, W)
    near = pltpu.roll(ext_ref[part, pl.ds(row, W), :], shift, 1)
    far = pltpu.roll(ext_ref[2 + part, pl.ds(row, W), :], shift, 1)
    return jnp.where(lane < W - col, near, far)


def forward_kernel(offsets_ref, ext_ref, probe_ref, right_ref, left_ref, far_ref, win_ref):
    def one(p, carried):
        row = offsets_ref[2 * p]
        col = offsets_ref[2 * p + 1]
        win_re = cut_window(ext_ref, 0, row, col)
        win_im = cut_window(ext_ref, 1, row, col)
        win_ref[p, 0] = win_re
        win_ref[p, 1] = win_im
        waves = []
        for m in range(MODES):
            probe_re, probe_im = probe_ref[2 * m], probe_ref[2 * m + 1]
            waves.append(
                jnp.concatenate(
                    [probe_re * win_re - probe_im * win_im, probe_re * win_im + probe_im * win_re],
                    axis=1,
                )
            )
        half_done = right_by(jnp.concatenate(waves, axis=0), right_ref[...])
        far_ref[p] = left_by(left_ref[...], swap_blocks(half_done))
        return carried

    lax.fori_loop(0, POSITIONS, one, 0, unroll=2)


def descan_of(sums, row, col):
    lane = lane_iota(sums.shape)
    pick = [
        jnp.sum(jnp.where(lane == i, sums, 0.0), axis=1, keepdims=True) for i in range(12)
    ]
    weight = pick[0]
    mean_row, mean_col = pick[1] / weight, pick[2] / weight
    var_row = pick[3] - mean_row * pick[1]
    var_both = pick[4] - mean_row * pick[2]
    var_col = pick[5] - mean_col * pick[2]
    determ = var_row * var_col - var_both * var_both
    shifts = []
    for first in (6, 9):
        tilt, tilt_row, tilt_col = pick[first : first + 3]
        cov_row = tilt_row - mean_row * tilt
        cov_col = tilt_col - mean_col * tilt
        slope_row = (var_col * cov_row - var_both * cov_col) / determ
        slope_col = (var_row * cov_col - var_both * cov_row) / determ
        shifts.append(tilt / weight + slope_row * (row - mean_row) + slope_col * (col - mean_col))
    return shifts


def circulant(line):
    return pltpu.roll(jnp.broadcast_to(line, (W, W)), 0, 1, stride=1, stride_axis=0)


def backward_kernel(
    row_dev,
    col_dev,
    offsets_ref,
    place_ref,
    sums_ref,
    patterns_ref,
    far_ref,
    win_ref,
    probe_ref,
    shift_ref,
    right_ref,
    left_ref,
    object_grad_ref,
    probe_grad_ref,
    cols_ref,
    rows_ref,
    nyquist_ref,
):
    sums = jnp.sum(sums_ref[...], axis=0, keepdims=True)
    row, col = place_of(place_ref, row_dev, col_dev, (POSITIONS, W))
    shift_row, shift_col = descan_of(sums, row, col)
    lane = lane_iota((POSITIONS, W))
    freq = jnp.where(lane <= HALF, lane, lane - HALF).astype(f32)
    quarter = jnp.where(lane <= HALF, 0.0, 0.25)

    def wave(shift):
        turns = freq * shift * (1.0 / W) + quarter
        return jnp.cos(2.0 * math.pi * (turns - jnp.round(turns)))

    def half_sine(shift):
        turns = shift * 0.5
        return jnp.sin(2.0 * math.pi * (turns - jnp.round(turns)))

    cols_ref[...] = jnp.dot(wave(shift_col), shift_ref[0], precision=highest)
    rows_ref[...] = jnp.dot(wave(shift_row), shift_ref[1], precision=highest)
    nyquist_ref[...] = half_sine(shift_row) * half_sine(shift_col) * (1.0 / (W * W))
    object_grad_ref[...] = jnp.zeros(object_grad_ref.shape, f32)
    probe_grad_ref[...] = jnp.zeros(probe_grad_ref.shape, f32)

    def one(p, carried):
        pattern = patterns_ref[p]
        place = row_iota((W, W)) + lane_iota((W, W))
        sign = (1 - 2 * (place & 1)).astype(f32)
        along_cols = circulant(cols_ref[pl.ds(p, 1), :])
        along_rows = circulant(rows_ref[pl.ds(p, 1), :])
        moved = jnp.dot(pattern, along_cols, precision=highest)
        moved = jnp.dot(along_rows, moved, precision=highest)
        alternate = jnp.sum(jnp.sum(pattern * sign, axis=0, keepdims=True), axis=1, keepdims=True)
        moved = moved - sign * (alternate * nyquist_ref[pl.ds(p, 1), :])
        target = jnp.sqrt(jnp.maximum(moved, 0.0))
        far = far_ref[p]
        power = far[:W, :W] ** 2 + far[:W, W:] ** 2 + far[W:, :W] ** 2 + far[W:, W:] ** 2
        factor = 1.0 - target / jnp.maximum(jnp.sqrt(power), amp_floor)
        wide = jnp.concatenate([factor, factor], axis=1)
        scaled = far * jnp.concatenate([wide, wide], axis=0)
        half_done = left_by(left_ref[...], scaled)
        back = right_by(swap_blocks(half_done), right_ref[...])
        win_re, win_im = win_ref[p, 0], win_ref[p, 1]
        grad_re = jnp.zeros((W, W), f32)
        grad_im = jnp.zeros((W, W), f32)
        for m in range(MODES):
            back_re, back_im = back[m * W : (m + 1) * W, :W], back[m * W : (m + 1) * W, W:]
            probe_re, probe_im = probe_ref[2 * m], probe_ref[2 * m + 1]
            grad_re += probe_re * back_re + probe_im * back_im
            grad_im += probe_re * back_im - probe_im * back_re
            probe_grad_ref[2 * m] += win_re * back_re + win_im * back_im
            probe_grad_ref[2 * m + 1] += win_re * back_im - win_im * back_re
        top = offsets_ref[2 * p]
        left = offsets_ref[2 * p + 1]
        lanes = lane_iota((W, W))
        for part, grad in enumerate((grad_re, grad_im)):
            turned = pltpu.roll(grad, left, 1)
            object_grad_ref[part, pl.ds(top, W), :] += jnp.where(lanes >= left, turned, 0.0)
            object_grad_ref[2 + part, pl.ds(top, W), :] += jnp.where(lanes < left, turned, 0.0)
        return carried

    lax.fori_loop(0, POSITIONS, one, 0)
    probe_power = (
        probe_ref[0] ** 2 + probe_ref[1] ** 2 + probe_ref[2] ** 2 + probe_ref[3] ** 2
    )
    peak = jnp.max(jnp.max(probe_power, axis=0, keepdims=True), axis=1, keepdims=True)
    object_grad_ref[...] = object_grad_ref[...] * (obj_rate / peak)[None]


def shifted_to(axis, step):
    count = lax.axis_size(axis)
    return [(i, (i + step) % count) for i in range(count)]


def spread(values, axis):
    return lax.all_to_all(values, axis, 0, 0, tiled=True)


SMEM = pl.BlockSpec(memory_space=pltpu.SMEM)
VMEM = pl.BlockSpec(memory_space=pltpu.VMEM)


def params(mib):
    return pltpu.CompilerParams(vmem_limit_bytes=mib * 1024 * 1024)


def on_device(patterns, offsets, object_field, probe):
    row_dev = lax.axis_size("srow")
    col_dev = lax.axis_size("scol")
    place = jnp.stack([lax.axis_index("srow"), lax.axis_index("scol")]).astype(jnp.int32)
    patterns = patterns.reshape(POSITIONS, W, W)
    offsets = offsets.reshape(2 * POSITIONS)
    probe_flat = probe.reshape(2 * MODES, W, W)
    right_fwd, left_fwd, right_inv, left_inv = (jnp.asarray(t) for t in dft_tables())
    shifts = jnp.asarray(shift_tables())

    above = lax.ppermute(object_field[:, TILE - HALF :, :], "srow", shifted_to("srow", 1))
    below = lax.ppermute(object_field[:, :HALF, :], "srow", shifted_to("srow", -1))

    sums = pl.pallas_call(
        lambda *refs: sums_kernel(row_dev, col_dev, *refs),
        out_shape=jax.ShapeDtypeStruct((row_dev, W), f32),
        in_specs=[SMEM, VMEM],
        out_specs=VMEM,
        scratch_shapes=[pltpu.VMEM((POSITIONS, W), f32), pltpu.VMEM((POSITIONS, W), f32)],
        compiler_params=params(8),
        name="sums",
    )(place, patterns)
    sums = spread(sums, "srow")

    tall = jnp.concatenate([above, object_field, below], axis=1)
    left_rim = lax.ppermute(tall[:, :, TILE - HALF :], "scol", shifted_to("scol", 1))
    right_rim = lax.ppermute(tall[:, :, :HALF], "scol", shifted_to("scol", -1))

    sums = jnp.broadcast_to(jnp.sum(sums, axis=0, keepdims=True), (col_dev, W))
    sums = spread(sums, "scol")

    near = jnp.concatenate([left_rim, tall[:, :, :HALF]], axis=2)
    blank = jnp.zeros((2, EXT, 2 * W - EXT), f32)
    far = jnp.concatenate([tall[:, :, HALF:], right_rim, blank], axis=2)
    ext = jnp.concatenate([near, far], axis=0)

    far, windows = pl.pallas_call(
        forward_kernel,
        out_shape=(
            jax.ShapeDtypeStruct((POSITIONS, 2 * W, 2 * W), f32),
            jax.ShapeDtypeStruct((POSITIONS, 2, W, W), f32),
        ),
        in_specs=[SMEM, VMEM, VMEM, VMEM, VMEM],
        out_specs=(VMEM, VMEM),
        compiler_params=params(24),
        name="forward",
    )(offsets, ext, probe_flat, right_fwd, left_fwd)

    ext_grad, probe_grad = pl.pallas_call(
        lambda *refs: backward_kernel(row_dev, col_dev, *refs),
        out_shape=(
            jax.ShapeDtypeStruct((4, EXT, W), f32),
            jax.ShapeDtypeStruct((2 * MODES, W, W), f32),
        ),
        in_specs=[SMEM, SMEM] + [VMEM] * 8,
        out_specs=(VMEM, VMEM),
        scratch_shapes=[pltpu.VMEM((POSITIONS, W), f32)] * 3,
        compiler_params=params(24),
        name="backward",
    )(offsets, place, sums, patterns, far, windows, probe_flat, shifts, right_inv, left_inv)

    from_below = lax.ppermute(ext_grad[:, :HALF, :], "srow", shifted_to("srow", -1))
    from_above = lax.ppermute(ext_grad[:, HALF + TILE :, :], "srow", shifted_to("srow", 1))

    chunk = 2 * MODES * W // row_dev
    parts = spread(probe_grad.reshape(row_dev, chunk, W), "srow")

    grad = ext_grad[:, HALF : HALF + TILE, :]
    grad = grad + jnp.pad(from_below, ((0, 0), (TILE - HALF, 0), (0, 0)))
    grad = grad + jnp.pad(from_above, ((0, 0), (0, TILE - HALF), (0, 0)))
    from_right = lax.ppermute(grad[:2, :, :HALF], "scol", shifted_to("scol", -1))
    from_left = lax.ppermute(
        grad[2:, :, TILE - HALF : TILE], "scol", shifted_to("scol", 1)
    )

    part = jnp.sum(parts, axis=0)
    part = spread(jnp.broadcast_to(part[None], (col_dev, chunk, W)), "scol")
    part = jnp.sum(part, axis=0)
    total = spread(jnp.broadcast_to(part[None], (row_dev, chunk, W)), "srow")

    grad = jnp.concatenate([grad[:2, :, HALF:], grad[2:, :, : TILE - HALF]], axis=2)
    grad = grad + jnp.pad(from_right, ((0, 0), (0, 0), (TILE - HALF, 0)))
    grad = grad + jnp.pad(from_left, ((0, 0), (0, 0), (0, TILE - HALF)))
    new_object = object_field - grad

    positions_all = POSITIONS * row_dev * col_dev
    new_probe = probe - (probe_rate / positions_all) * total.reshape(probe.shape)
    return new_object, new_probe


def solution(mesh):
    placed = (P("srow", "scol", None, None), P("srow", "scol", None), P(None, "srow", "scol"), P())
    return jax.shard_map(
        on_device,
        mesh=mesh,
        in_specs=placed,
        out_specs=(P(None, "srow", "scol"), P()),
        check_vma=False,
    )
```

time: 762 us -> 130 us (0.17)
  waiting for transfers between devices: 253 us -> 29.9 us
  blocking collectives: 152 us -> 0 us
  loops' own time: 122 us -> 0 us
  matrix products: 93.4 us -> 0 us
  local copies, waits for them, and re-layouts: 83.1 us -> 17 us
  starting transfers between devices: 15.6 us -> 47.2 us
  Pallas kernels: 0 us -> 30.9 us
  between operations: 21.2 us -> 0.87 us
  other arithmetic: 16.3 us -> 2.78 us
    psum x1 -> x0, waiting for transfers between devices: 238 us -> none  [on_device(): summed = lax.psum(probe_grad, ('srow', 'scol'))]
    psum x2 -> x0, blocking collectives: 152 us -> none  [the longest x1 78.5 us: on_device(): lax.psum((first_sums, centre_moment), ('srow', 'scol'))]
    another operation x2 -> x0, loops' own time: 122 us -> none  [the longest x1 62.7 us: on_device(): lax.fori_loop(0, position_count, add_one, jnp.zeros(extended.shape, jnp.f...]
    dot_general x35 -> x0, matrix products: 93.4 us -> none  [the longest x14 51.1 us: rows_by(): return jnp.einsum('uk,...kv->...uv', matrix, values, precision=highest)]
    dynamic_slice x64 -> x0, local copies, waits for them, and re-layouts: 38.6 us -> none  [the longest x32 19.8 us: cut_one(): corner = (jnp.int32(0), row_start[place], col_start[place])]
    dynamic_update_slice x32 -> x0, local copies, waits for them, and re-layouts: 37.5 us -> none  [the longest x16 35.7 us: add_one(): return lax.dynamic_update_slice(accum, current + grad_stack[place], corner)]
    pallas_call x0 -> x3, Pallas kernels: none -> 30.9 us  [the longest x1 21.2 us: on_device(): pl.pallas_call(lambda *refs: backward_kernel(row_dev, col_dev, *refs), ou...]
    all_to_all x0 -> x5, starting transfers between devices: none -> 30.6 us  [spread(): return lax.all_to_all(values, axis, 0, 0, tiled=True)]
  transfers between devices with their start and end apart: 9 -> 13, of which waited for: 5 -> 6; matrix products, arithmetic and copies ran while one was open for 6% -> 6% of each run, Pallas kernels for 0% -> 8%
where the time goes in v1:
time: 130 us; the launch traced here: 129 us
  starting transfers between devices  47.2 us (36%)
  Pallas kernels  30.9 us (24%)
  waiting for transfers between devices  29.9 us (23%)
  local copies, waits for them, and re-layouts  17 us (13%)
  other arithmetic  2.78 us (2%)
    all_to_all x5, starting transfers between devices, spread(): return lax.all_to_all(values, axis, 0, 0, tiled=True)  30.6 us
    all_to_all x5, waiting for transfers between devices, spread(): return lax.all_to_all(values, axis, 0, 0, tiled=True)  24.9 us
    pallas_call x1, Pallas kernels, on_device(): pl.pallas_call(lambda *refs: backward_kernel(row_dev, col_dev, *refs), ou...  21.2 us
    unnamed x29, local copies, waits for them, and re-layouts  12.5 us
    pallas_call x1, Pallas kernels, on_device(): pl.pallas_call(forward_kernel, out_shape=(jax.ShapeDtypeStruct((POSITIONS...  8.33 us
    ppermute x1, starting transfers between devices, on_device(): right_rim = lax.ppermute(tall[:, :, :HALF], 'scol', shifted_to('scol', -1))  5.28 us
    ppermute x1, starting transfers between devices, on_device(): lax.ppermute(object_field[:, TILE - HALF:, :], 'srow', shifted_to('srow',...  4.38 us
    ppermute x1, waiting for transfers between devices, on_device(): lax.ppermute(object_field[:, :HALF, :], 'srow', shifted_to('srow', -1))  3.67 us
  transfers between devices with their start and end apart: 13, of which 6 were waited for; matrix products, arithmetic and copies ran while one was open for 6% of the time, Pallas kernels for 8%

profile of v1, /device:TPU:1, one launch (start us, length us, event | category | flops | bytes accessed | tf_op | source)
XLA Modules:
  0.0 128.8 jit_solution(9812949495559172085)
XLA Ops:
  0.7 1.0 fusion.5
  1.7 4.4 %collective-permute-start = (f32[2,64,72]{2,1,0:T(8,128)S(1)}, f32[2,64,72]{2,1,0:T(8,128)S(1)}, u32[]{:S(2)}, u32[]{:S(2)}) collective-permute-start(f32[2,64,72]{2,1,0:T(8,128)S(1)} %get-tuple-element.18), channel_id=1, source_target_pairs={{0,16},{16,32},{32,48},{48,64},{64,80},{80,96},{96,112},{112,128},... | collective-permute-start | bytes 110600 | tf_op jit(solution)/shard_map/ppermute | solution.py:300
  6.0 1.3 %collective-permute-done = f32[2,64,72]{2,1,0:T(8,128)S(1)} collective-permute-done((f32[2,64,72]{2,1,0:T(8,128)S(1)}, f32[2,64,72]{2,1,0:T(8,128)S(1)}, u32[]{:S(2)}, u32[]{:S(2)}) %collective-permute-start) | collective-permute-done | bytes 36896 | tf_op jit(solution)/shard_map/ppermute | solution.py:300
  8.3 3.7 %collective-permute-done.1 = f32[2,64,72]{2,1,0:T(8,128)S(1)} collective-permute-done((f32[2,64,72]{2,1,0:T(8,128)S(1)}, f32[2,64,72]{2,1,0:T(8,128)S(1)}, u32[]{:S(2)}, u32[]{:S(2)}) %collective-permute-start.1) | collective-permute-done | bytes 36896 | tf_op jit(solution)/shard_map/ppermute | solution.py:301
  12.2 5.3 %collective-permute-start.3 = (f32[2,200,64]{2,1,0:T(8,128)S(1)}, f32[2,200,64]{2,1,0:T(8,128)S(1)}, u32[]{:S(2)}, u32[]{:S(2)}) collective-permute-start(f32[2,200,64]{2,1,0:T(8,128)S(1)} %get-tuple-element.13), channel_id=1, source_target_pairs={{0,15},{1,0},{2,1},{3,2},{4,3},{5,4},{6,5},{7,6},{8,7},{9,8},{10,9... | collective-permute-start | bytes 307208 | tf_op jit(solution)/shard_map/ppermute | solution.py:316
  17.5 1.2 copy-done.2
  18.7 1.4 %sums.1 = f32[16,128]{1,0:T(8,128)} custom-call(s32[2]{0:T(128)S(1)} %pad_add_fusion.1.refs_0_.refs_1_, f32[16,128,128]{2,1,0:T(8,128)S(1)} %bitcast.10), custom_call_target="tpu_custom_call" | custom-call | tf_op jit(solution)/shard_map/sums/pallas_call | solution.py:303
  20.1 7.2 %all-to-all-start = ((f32[16,1,128]{2,1,0:T(1,128)}), f32[16,1,128]{2,1,0:T(1,128)S(1)}, u32[]{:S(2)}, u32[]{:S(2)}) async-start(f32[16,1,128]{2,1,0:T(1,128)} %bitcast.4), calls=%async_computation | async-start | bytes 16384 | tf_op jit(solution)/shard_map/all_to_all | solution.py:279
  28.3 5.9 %all-to-all-done = f32[16,1,128]{2,1,0:T(1,128)S(1)} async-done(((f32[16,1,128]{2,1,0:T(1,128)}), f32[16,1,128]{2,1,0:T(1,128)S(1)}, u32[]{:S(2)}, u32[]{:S(2)}) %all-to-all-start) | async-done | bytes 8224 | tf_op jit(solution)/shard_map/all_to_all | solution.py:279
  34.9 4.6 %all-to-all-start.1 = ((f32[16,1,128]{2,1,0:T(1,128)}), f32[16,1,128]{2,1,0:T(1,128)S(1)}, u32[]{:S(2)}, u32[]{:S(2)}) async-start(f32[16,1,128]{2,1,0:T(1,128)} %broadcast_in_dim.8), calls=%async_computation.1 | async-start | bytes 16384 | tf_op jit(solution)/shard_map/all_to_all | solution.py:279
  40.8 1.0 copy-done.7
  41.8 8.3 %forward.1 = (f32[16,256,256]{2,1,0:T(8,128)S(1)}, f32[16,2,128,128]{3,2,1,0:T(8,128)S(1)}) custom-call(s32[32]{0:T(128)S(1)} %reshape.29.offsets_ref.refs_0_, f32[4,200,128]{2,1,0:T(8,128)S(1)} %maximum_maximum_fusion.ext_ref, f32[4,128,128]{2,1,0:T(8,128)S(1)} %bitcast.12, bf16[768,256]{1,0:T(8,128)(2,1)S(1)} %copy-done.7, bf16[256,768]{1,0:T(8,128)(2,1)S(1)} %copy-done.6), custom_call_target="tpu_custom_call" | custom-call | tf_op jit(solution)/shard_map/forward/pallas_call | solution.py:326
  50.2 1.9 %copy-done = f32[16,256,256]{2,1,0:T(8,128)} copy-done((f32[16,256,256]{2,1,0:T(8,128)}, f32[16,256,256]{2,1,0:T(8,128)S(1)}, u32[]{:S(2)}) %copy-start) | copy-done | bytes 4194328
  52.1 2.2 %copy-done.1 = f32[16,256,256]{2,1,0:T(8,128)S(1)} copy-done((f32[16,256,256]{2,1,0:T(8,128)S(1)}, f32[16,256,256]{2,1,0:T(8,128)}, u32[]{:S(2)}) %copy-start.1) | copy-done | bytes 4194328
  54.3 1.0 copy-done.8
  56.3 21.2 %backward.1 = (f32[4,200,128]{2,1,0:T(8,128)S(1)}, f32[4,128,128]{2,1,0:T(8,128)S(1)}) custom-call(s32[32]{0:T(128)S(1)} %reshape.29.offsets_ref.refs_0_, s32[2]{0:T(128)S(1)} %pad_add_fusion.1.refs_0_.refs_1_, f32[16,128]{1,0:T(8,128)S(1)} %bitcast.15, f32[16,128,128]{2,1,0:T(8,128)S(1)} %bitcast.11, f32[16,256,256]{2,1,0:T(8,128)S(1)} %copy-done.1, ...), custom_call_target="tpu_custom_call" | custom-call | tf_op jit(solution)/shard_map/backward/pallas_call | solution.py:338
  79.0 4.4 %all-to-all-start.2 = ((f32[16,32,128]{2,1,0:T(8,128)}), f32[16,32,128]{2,1,0:T(8,128)S(1)}, u32[]{:S(2)}, u32[]{:S(2)}) async-start(f32[16,32,128]{2,1,0:T(8,128)} %bitcast.14), calls=%async_computation.2 | async-start | bytes 524288 | tf_op jit(solution)/shard_map/all_to_all | solution.py:279
  84.7 3.0 %collective-permute-start.5 = (f32[4,64,128]{2,1,0:T(8,128)S(1)}, f32[4,64,128]{2,1,0:T(8,128)S(1)}, u32[]{:S(2)}, u32[]{:S(2)}) collective-permute-start(f32[4,64,128]{2,1,0:T(8,128)S(1)} %get-tuple-element.11), channel_id=1, source_target_pairs={{0,16},{16,32},{32,48},{48,64},{64,80},{80,96},{96,112},{112,128},... | collective-permute-start | bytes 393224 | tf_op jit(solution)/shard_map/ppermute | solution.py:352
  87.7 4.6 %all-to-all-done.2 = f32[16,32,128]{2,1,0:T(8,128)S(1)} async-done(((f32[16,32,128]{2,1,0:T(8,128)}), f32[16,32,128]{2,1,0:T(8,128)S(1)}, u32[]{:S(2)}, u32[]{:S(2)}) %all-to-all-start.2) | async-done | bytes 262176 | tf_op jit(solution)/shard_map/all_to_all | solution.py:279
  93.1 7.8 %all-to-all-start.3 = ((f32[16,32,128]{2,1,0:T(8,128)}), f32[16,32,128]{2,1,0:T(8,128)S(1)}, u32[]{:S(2)}, u32[]{:S(2)}) async-start(f32[16,32,128]{2,1,0:T(8,128)} %broadcast_in_dim.10), calls=%async_computation.3 | async-start | bytes 524288 | tf_op jit(solution)/shard_map/all_to_all | solution.py:279
  102.1 3.6 %collective-permute-start.6 = (f32[2,72,64]{2,1,0:T(8,128)S(1)}, f32[2,72,64]{2,1,0:T(8,128)S(1)}, u32[]{:S(2)}, u32[]{:S(2)}) collective-permute-start(f32[2,72,64]{2,1,0:T(8,128)S(1)} %get-tuple-element.14), channel_id=1, source_target_pairs={{0,15},{1,0},{2,1},{3,2},{4,3},{5,4},{6,5},{7,6},{8,7},{9,8},{10,9... | collective-permute-start | bytes 110600 | tf_op jit(solution)/shard_map/ppermute | solution.py:360
  105.6 6.2 %all-to-all-done.3 = f32[16,32,128]{2,1,0:T(8,128)S(1)} async-done(((f32[16,32,128]{2,1,0:T(8,128)}), f32[16,32,128]{2,1,0:T(8,128)S(1)}, u32[]{:S(2)}, u32[]{:S(2)}) %all-to-all-start.3) | async-done | bytes 262176 | tf_op jit(solution)/shard_map/all_to_all | solution.py:279
  112.6 6.5 %all-to-all-start.4 = ((f32[16,32,128]{2,1,0:T(8,128)}), f32[16,32,128]{2,1,0:T(8,128)S(1)}, u32[]{:S(2)}, u32[]{:S(2)}) async-start(f32[16,32,128]{2,1,0:T(8,128)} %broadcast_in_dim.11), calls=%async_computation.4 | async-start | bytes 524288 | tf_op jit(solution)/shard_map/all_to_all | solution.py:279
  119.9 8.1 %all-to-all-done.4 = f32[16,32,128]{2,1,0:T(8,128)S(1)} async-done(((f32[16,32,128]{2,1,0:T(8,128)}), f32[16,32,128]{2,1,0:T(8,128)S(1)}, u32[]{:S(2)}, u32[]{:S(2)}) %all-to-all-start.4) | async-done | bytes 262176 | tf_op jit(solution)/shard_map/all_to_all | solution.py:279
  (56 shorter events, 11.9 us)
Async XLA Ops:
  0.6 51.5 %copy-start.11 = (f32[2,128,128]{2,1,0:T(8,128)S(1)}, f32[2,128,128]{2,1,0:T(8,128)}, u32[]{:S(2)}) copy-start(f32[2,128,128]{2,1,0:T(8,128)} %constant.28.clone.refs_7_) | copy-start | bytes 393220
  0.6 51.5 %copy-start.3 = (f32[4,4,128,128]{3,2,1,0:T(8,128)S(1)}, f32[4,4,128,128]{3,2,1,0:T(8,128)}, u32[]{:S(2)}) copy-start(f32[4,4,128,128]{3,2,1,0:T(8,128)} %param.9) | copy-start | bytes 3145732
  0.7 39.2 %copy-start.4 = (f32[2,2,128,128]{3,2,1,0:T(8,128)S(1)}, f32[2,2,128,128]{3,2,1,0:T(8,128)}, u32[]{:S(2)}) copy-start(f32[2,2,128,128]{3,2,1,0:T(8,128)} %param.12) | copy-start | bytes 786436
  1.7 5.7 %collective-permute-start = (f32[2,64,72]{2,1,0:T(8,128)S(1)}, f32[2,64,72]{2,1,0:T(8,128)S(1)}, u32[]{:S(2)}, u32[]{:S(2)}) collective-permute-start(f32[2,64,72]{2,1,0:T(8,128)S(1)} %get-tuple-element.18), channel_id=1, source_target_pairs={{0,16},{16,32},{32,48},{48,64},{64,80},{80,96},{96,112},{112,128},... | collective-permute-start | bytes 110600 | tf_op jit(solution)/shard_map/ppermute | solution.py:300
  6.0 5.9 %collective-permute-start.1 = (f32[2,64,72]{2,1,0:T(8,128)S(1)}, f32[2,64,72]{2,1,0:T(8,128)S(1)}, u32[]{:S(2)}, u32[]{:S(2)}) collective-permute-start(f32[2,64,72]{2,1,0:T(8,128)S(1)} %get-tuple-element.17), channel_id=1, source_target_pairs={{0,240},{16,0},{32,16},{48,32},{64,48},{80,64},{96,80},{112,96},{1... | collective-permute-start | bytes 110600 | tf_op jit(solution)/shard_map/ppermute | solution.py:301
  12.1 27.6 %collective-permute-start.2 = (f32[2,200,64]{2,1,0:T(8,128)S(1)}, f32[2,200,64]{2,1,0:T(8,128)S(1)}, u32[]{:S(2)}, u32[]{:S(2)}) collective-permute-start(f32[2,200,64]{2,1,0:T(8,128)S(1)} %get-tuple-element.12), channel_id=1, source_target_pairs={{0,1},{1,2},{2,3},{3,4},{4,5},{5,6},{6,7},{7,8},{8,9},{9,10},{10,1... | collective-permute-start | bytes 307208 | tf_op jit(solution)/shard_map/ppermute | solution.py:315
  12.2 27.5 %collective-permute-start.3 = (f32[2,200,64]{2,1,0:T(8,128)S(1)}, f32[2,200,64]{2,1,0:T(8,128)S(1)}, u32[]{:S(2)}, u32[]{:S(2)}) collective-permute-start(f32[2,200,64]{2,1,0:T(8,128)S(1)} %get-tuple-element.13), channel_id=1, source_target_pairs={{0,15},{1,0},{2,1},{3,2},{4,3},{5,4},{6,5},{7,6},{8,7},{9,8},{10,9... | collective-permute-start | bytes 307208 | tf_op jit(solution)/shard_map/ppermute | solution.py:316
  17.5 1.2 copy-start.2
  20.1 14.2 %all-to-all-start = ((f32[16,1,128]{2,1,0:T(1,128)}), f32[16,1,128]{2,1,0:T(1,128)S(1)}, u32[]{:S(2)}, u32[]{:S(2)}) async-start(f32[16,1,128]{2,1,0:T(1,128)} %bitcast.4), calls=%async_computation | async-start | bytes 16384 | tf_op jit(solution)/shard_map/all_to_all | solution.py:279
  34.9 17.2 %all-to-all-start.1 = ((f32[16,1,128]{2,1,0:T(1,128)}), f32[16,1,128]{2,1,0:T(1,128)S(1)}, u32[]{:S(2)}, u32[]{:S(2)}) async-start(f32[16,1,128]{2,1,0:T(1,128)} %broadcast_in_dim.8), calls=%async_computation.1 | async-start | bytes 16384 | tf_op jit(solution)/shard_map/all_to_all | solution.py:279
  39.8 1.0 copy-start.6
  40.8 1.0 copy-start.7
  50.2 1.9 %copy-start = (f32[16,256,256]{2,1,0:T(8,128)}, f32[16,256,256]{2,1,0:T(8,128)S(1)}, u32[]{:S(2)}) copy-start(f32[16,256,256]{2,1,0:T(8,128)S(1)} %get-tuple-element.6.refs_4_) | copy-start | bytes 12582916
  52.1 2.2 %copy-start.1 = (f32[16,256,256]{2,1,0:T(8,128)S(1)}, f32[16,256,256]{2,1,0:T(8,128)}, u32[]{:S(2)}) copy-start(f32[16,256,256]{2,1,0:T(8,128)} %copy-done) | copy-start | bytes 12582916
  54.3 1.0 copy-start.8
  55.3 1.0 copy-start.9
  79.0 40.1 %copy-start.12 = (f32[2,72,72]{2,1,0:T(8,128)S(1)}, f32[2,72,72]{2,1,0:T(8,128)}, u32[]{:S(2)}) copy-start(f32[2,72,72]{2,1,0:T(8,128)} %param.11) | copy-start | bytes 124420
  79.0 13.4 %all-to-all-start.2 = ((f32[16,32,128]{2,1,0:T(8,128)}), f32[16,32,128]{2,1,0:T(8,128)S(1)}, u32[]{:S(2)}, u32[]{:S(2)}) async-start(f32[16,32,128]{2,1,0:T(8,128)} %bitcast.14), calls=%async_computation.2 | async-start | bytes 524288 | tf_op jit(solution)/shard_map/all_to_all | solution.py:279
  84.4 16.6 %collective-permute-start.4 = (f32[4,64,128]{2,1,0:T(8,128)S(1)}, f32[4,64,128]{2,1,0:T(8,128)S(1)}, u32[]{:S(2)}, u32[]{:S(2)}) collective-permute-start(f32[4,64,128]{2,1,0:T(8,128)S(1)} %get-tuple-element.10), channel_id=1, source_target_pairs={{0,240},{16,0},{32,16},{48,32},{64,48},{80,64},{96,80},{112,96},{1... | collective-permute-start | bytes 393224 | tf_op jit(solution)/shard_map/ppermute | solution.py:351
  84.7 16.3 %collective-permute-start.5 = (f32[4,64,128]{2,1,0:T(8,128)S(1)}, f32[4,64,128]{2,1,0:T(8,128)S(1)}, u32[]{:S(2)}, u32[]{:S(2)}) collective-permute-start(f32[4,64,128]{2,1,0:T(8,128)S(1)} %get-tuple-element.11), channel_id=1, source_target_pairs={{0,16},{16,32},{32,48},{48,64},{64,80},{80,96},{96,112},{112,128},... | collective-permute-start | bytes 393224 | tf_op jit(solution)/shard_map/ppermute | solution.py:352
  93.1 18.7 %all-to-all-start.3 = ((f32[16,32,128]{2,1,0:T(8,128)}), f32[16,32,128]{2,1,0:T(8,128)S(1)}, u32[]{:S(2)}, u32[]{:S(2)}) async-start(f32[16,32,128]{2,1,0:T(8,128)} %broadcast_in_dim.10), calls=%async_computation.3 | async-start | bytes 524288 | tf_op jit(solution)/shard_map/all_to_all | solution.py:279
  102.1 17.1 %collective-permute-start.6 = (f32[2,72,64]{2,1,0:T(8,128)S(1)}, f32[2,72,64]{2,1,0:T(8,128)S(1)}, u32[]{:S(2)}, u32[]{:S(2)}) collective-permute-start(f32[2,72,64]{2,1,0:T(8,128)S(1)} %get-tuple-element.14), channel_id=1, source_target_pairs={{0,15},{1,0},{2,1},{3,2},{4,3},{5,4},{6,5},{7,6},{8,7},{9,8},{10,9... | collective-permute-start | bytes 110600 | tf_op jit(solution)/shard_map/ppermute | solution.py:360
  105.6 13.5 %collective-permute-start.7 = (f32[2,72,64]{2,1,0:T(8,128)S(1)}, f32[2,72,64]{2,1,0:T(8,128)S(1)}, u32[]{:S(2)}, u32[]{:S(2)}) collective-permute-start(f32[2,72,64]{2,1,0:T(8,128)S(1)} %get-tuple-element.15), channel_id=1, source_target_pairs={{0,1},{1,2},{2,3},{3,4},{4,5},{5,6},{6,7},{7,8},{8,9},{9,10},{10,1... | collective-permute-start | bytes 110600 | tf_op jit(solution)/shard_map/ppermute | solution.py:361
  112.6 15.4 %all-to-all-start.4 = ((f32[16,32,128]{2,1,0:T(8,128)}), f32[16,32,128]{2,1,0:T(8,128)S(1)}, u32[]{:S(2)}, u32[]{:S(2)}) async-start(f32[16,32,128]{2,1,0:T(8,128)} %broadcast_in_dim.11), calls=%async_computation.4 | async-start | bytes 524288 | tf_op jit(solution)/shard_map/all_to_all | solution.py:279
  (2 other events, 1.5 us)

commit v2 on v1

--- a/solution.py
+++ b/solution.py
@@ -17,6 +17,8 @@
 POSITIONS = PR * PC
 TILE = 72
 EXT = TILE + W
+GROUP = 4
+AHEAD = 8
 
 obj_rate = 0.2
 probe_rate = 0.5
@@ -29,19 +31,11 @@
 def dft_tables():
     counter = np.arange(W)
     angles = 2.0 * np.pi / W * (counter[:, None] * counter[None, :] % W)
-    cos, sin = np.cos(angles), np.sin(angles)
-    pair = np.block([[cos, -sin], [sin, cos]])
-
-    def parts(matrix, axis):
-        high = matrix.astype(ml_dtypes.bfloat16)
-        low = (matrix - high.astype(np.float64)).astype(ml_dtypes.bfloat16)
-        return np.concatenate([high, high, low], axis=axis)
-
-    right_fwd = parts(pair / 16, 0)
-    left_fwd = parts(pair.T / 8, 1)
-    right_inv = parts(pair.T / 16, 0)
-    left_inv = parts(pair / 8, 1)
-    return right_fwd, left_fwd, right_inv, left_inv
+    parts = []
+    for table in (np.cos(angles), np.sin(angles)):
+        high = table.astype(ml_dtypes.bfloat16)
+        parts += [high, (table - high.astype(np.float64)).astype(ml_dtypes.bfloat16)]
+    return np.stack(parts)
 
 
 def shift_tables():
@@ -59,6 +53,33 @@
     high = values.astype(bf16)
     low = (values - high.astype(f32)).astype(bf16)
     return high, low
+
+
+def fill_tables(tables_ref, right_ref, left_ref, inverse):
+    for part in range(3):
+        cos = tables_ref[part // 2]
+        sin = tables_ref[2 + part // 2]
+        plus, minus = (sin, -sin) if inverse else (-sin, sin)
+        base = part * 2 * W
+        right_ref[base : base + W, 0:W] = cos
+        right_ref[base : base + W, W:] = plus
+        right_ref[base + W : base + 2 * W, 0:W] = minus
+        right_ref[base + W : base + 2 * W, W:] = cos
+        scale = jnp.asarray(1.0 / W, bf16)
+        left_ref[0:W, base : base + W] = cos * scale
+        left_ref[0:W, base + W : base + 2 * W] = minus * scale
+        left_ref[W:, base : base + W] = plus * scale
+        left_ref[W:, base + W : base + 2 * W] = cos * scale
+
+
+def by_parts(left, right):
+    high, low = split(left)
+    other_high, other_low = split(right)
+    return jnp.dot(
+        jnp.concatenate([high, low, high], axis=1),
+        jnp.concatenate([other_high, other_high, other_low], axis=0),
+        preferred_element_type=f32,
+    )
 
 
 def right_by(values, table):
@@ -135,28 +156,38 @@
     return jnp.where(lane < W - col, near, far)
 
 
-def forward_kernel(offsets_ref, ext_ref, probe_ref, right_ref, left_ref, far_ref, win_ref):
-    def one(p, carried):
-        row = offsets_ref[2 * p]
-        col = offsets_ref[2 * p + 1]
-        win_re = cut_window(ext_ref, 0, row, col)
-        win_im = cut_window(ext_ref, 1, row, col)
-        win_ref[p, 0] = win_re
-        win_ref[p, 1] = win_im
+def forward_kernel(
+    offsets_ref, ext_ref, probe_ref, tables_ref, far_out,
+    right_ref, left_ref, far_ref, far_sem,
+):
+    fill_tables(tables_ref, right_ref, left_ref, False)
+
+    def some(group, carried):
+        places = [group * GROUP + i for i in range(GROUP)]
         waves = []
-        for m in range(MODES):
-            probe_re, probe_im = probe_ref[2 * m], probe_ref[2 * m + 1]
-            waves.append(
-                jnp.concatenate(
-                    [probe_re * win_re - probe_im * win_im, probe_re * win_im + probe_im * win_re],
-                    axis=1,
-                )
-            )
+        for p in places:
+            row, col = offsets_ref[2 * p], offsets_ref[2 * p + 1]
+            win_re = cut_window(ext_ref, 0, row, col)
+            win_im = cut_window(ext_ref, 1, row, col)
+            for m in range(MODES):
+                probe_re, probe_im = probe_ref[2 * m], probe_ref[2 * m + 1]
+                wave_re = probe_re * win_re - probe_im * win_im
+                wave_im = probe_re * win_im + probe_im * win_re
+                waves.append(jnp.concatenate([wave_re, wave_im], axis=1))
         half_done = right_by(jnp.concatenate(waves, axis=0), right_ref[...])
-        far_ref[p] = left_by(left_ref[...], swap_blocks(half_done))
+        for i, p in enumerate(places):
+            mine = half_done[i * 2 * W : (i + 1) * 2 * W]
+            far_ref[p] = left_by(left_ref[...], swap_blocks(mine))
+        copy_of(group).start()
         return carried
 
-    lax.fori_loop(0, POSITIONS, one, 0, unroll=2)
+    def copy_of(group):
+        part = pl.ds(group * GROUP, GROUP)
+        return pltpu.make_async_copy(far_ref.at[part], far_out.at[part], far_sem.at[group])
+
+    lax.fori_loop(0, POSITIONS // GROUP, some, 0)
+    for group in range(POSITIONS // GROUP):
+        copy_of(group).wait()
 
 
 def descan_of(sums, row, col):
@@ -181,29 +212,28 @@
     return shifts
 
 
-def circulant(line):
-    return pltpu.roll(jnp.broadcast_to(line, (W, W)), 0, 1, stride=1, stride_axis=0)
+def seed_of(line):
+    return pltpu.roll(jnp.broadcast_to(line, (8, W)), 0, 1, stride=1, stride_axis=0)
+
+
+def circulant(seed):
+    return jnp.concatenate(
+        [seed if i == 0 else pltpu.roll(seed, 8 * i, 1) for i in range(W // 8)], axis=0
+    )
 
 
 def backward_kernel(
-    row_dev,
-    col_dev,
-    offsets_ref,
-    place_ref,
-    sums_ref,
-    patterns_ref,
-    far_ref,
-    win_ref,
-    probe_ref,
-    shift_ref,
-    right_ref,
-    left_ref,
-    object_grad_ref,
-    probe_grad_ref,
-    cols_ref,
-    rows_ref,
-    nyquist_ref,
+    row_dev, col_dev, offsets_ref, place_ref, sums_ref, patterns_ref, far_in, ext_ref, probe_ref,
+    shift_ref, tables_ref, object_grad_ref, probe_grad_ref,
+    cols_ref, rows_ref, nyquist_ref, right_ref, left_ref, target_ref, far_ref, far_sem,
 ):
+    far_copies = [
+        pltpu.make_async_copy(far_in.at[part], far_ref.at[part], far_sem.at[i])
+        for i, part in enumerate(pl.ds(i * GROUP, GROUP) for i in range(POSITIONS // GROUP))
+    ]
+    for copy in far_copies:
+        copy.start()
+
     sums = jnp.sum(sums_ref[...], axis=0, keepdims=True)
     row, col = place_of(place_ref, row_dev, col_dev, (POSITIONS, W))
     shift_row, shift_col = descan_of(sums, row, col)
@@ -219,50 +249,77 @@
         turns = shift * 0.5
         return jnp.sin(2.0 * math.pi * (turns - jnp.round(turns)))
 
-    cols_ref[...] = jnp.dot(wave(shift_col), shift_ref[0], precision=highest)
-    rows_ref[...] = jnp.dot(wave(shift_row), shift_ref[1], precision=highest)
+    cols = jnp.dot(wave(shift_col), shift_ref[0], precision=highest)
+    rows = jnp.dot(wave(shift_row), shift_ref[1], precision=highest)
+    for p in range(POSITIONS):
+        cols_ref[p] = seed_of(cols[p : p + 1])
+        rows_ref[p] = seed_of(rows[p : p + 1])
     nyquist_ref[...] = half_sine(shift_row) * half_sine(shift_col) * (1.0 / (W * W))
+    fill_tables(tables_ref, right_ref, left_ref, True)
     object_grad_ref[...] = jnp.zeros(object_grad_ref.shape, f32)
     probe_grad_ref[...] = jnp.zeros(probe_grad_ref.shape, f32)
 
-    def one(p, carried):
-        pattern = patterns_ref[p]
+    def make_targets(group, carried):
         place = row_iota((W, W)) + lane_iota((W, W))
         sign = (1 - 2 * (place & 1)).astype(f32)
-        along_cols = circulant(cols_ref[pl.ds(p, 1), :])
-        along_rows = circulant(rows_ref[pl.ds(p, 1), :])
-        moved = jnp.dot(pattern, along_cols, precision=highest)
-        moved = jnp.dot(along_rows, moved, precision=highest)
-        alternate = jnp.sum(jnp.sum(pattern * sign, axis=0, keepdims=True), axis=1, keepdims=True)
-        moved = moved - sign * (alternate * nyquist_ref[pl.ds(p, 1), :])
-        target = jnp.sqrt(jnp.maximum(moved, 0.0))
-        far = far_ref[p]
-        power = far[:W, :W] ** 2 + far[:W, W:] ** 2 + far[W:, :W] ** 2 + far[W:, W:] ** 2
-        factor = 1.0 - target / jnp.maximum(jnp.sqrt(power), amp_floor)
-        wide = jnp.concatenate([factor, factor], axis=1)
-        scaled = far * jnp.concatenate([wide, wide], axis=0)
-        half_done = left_by(left_ref[...], scaled)
-        back = right_by(swap_blocks(half_done), right_ref[...])
-        win_re, win_im = win_ref[p, 0], win_ref[p, 1]
-        grad_re = jnp.zeros((W, W), f32)
-        grad_im = jnp.zeros((W, W), f32)
+        for p in [group * AHEAD + i for i in range(AHEAD)]:
+            pattern = patterns_ref[p]
+            moved = by_parts(pattern, circulant(cols_ref[p]))
+            moved = by_parts(circulant(rows_ref[p]), moved)
+            alternate = jnp.sum(pattern * sign, axis=0, keepdims=True)
+            alternate = jnp.sum(alternate, axis=1, keepdims=True)
+            moved = moved - sign * (alternate * nyquist_ref[pl.ds(p, 1), :])
+            target_ref[p] = jnp.sqrt(jnp.maximum(moved, 0.0))
+        return carried
+
+    lax.fori_loop(0, POSITIONS // AHEAD, make_targets, 0)
+
+    def some(group, carried):
+        places = [group * GROUP + i for i in range(GROUP)]
+        halves = []
+        for p in places:
+            far = far_ref[p]
+            power = far[:W, :W] ** 2 + far[:W, W:] ** 2 + far[W:, :W] ** 2 + far[W:, W:] ** 2
+            factor = 1.0 - target_ref[p] / jnp.maximum(jnp.sqrt(power), amp_floor)
+            wide = jnp.concatenate([factor, factor], axis=1)
+            scaled = far * jnp.concatenate([wide, wide], axis=0)
+            halves.append(swap_blocks(left_by(left_ref[...], scaled)))
+        back = right_by(jnp.concatenate(halves, axis=0), right_ref[...])
+        lanes = lane_iota((W, W))
+        windows = []
+        for p in places:
+            at = offsets_ref[2 * p], offsets_ref[2 * p + 1]
+            windows.append((cut_window(ext_ref, 0, *at), cut_window(ext_ref, 1, *at)))
         for m in range(MODES):
-            back_re, back_im = back[m * W : (m + 1) * W, :W], back[m * W : (m + 1) * W, W:]
-            probe_re, probe_im = probe_ref[2 * m], probe_ref[2 * m + 1]
-            grad_re += probe_re * back_re + probe_im * back_im
-            grad_im += probe_re * back_im - probe_im * back_re
-            probe_grad_ref[2 * m] += win_re * back_re + win_im * back_im
-            probe_grad_ref[2 * m + 1] += win_re * back_im - win_im * back_re
-        top = offsets_ref[2 * p]
-        left = offsets_ref[2 * p + 1]
-        lanes = lane_iota((W, W))
-        for part, grad in enumerate((grad_re, grad_im)):
-            turned = pltpu.roll(grad, left, 1)
-            object_grad_ref[part, pl.ds(top, W), :] += jnp.where(lanes >= left, turned, 0.0)
-            object_grad_ref[2 + part, pl.ds(top, W), :] += jnp.where(lanes < left, turned, 0.0)
+            sum_re = jnp.zeros((W, W), f32)
+            sum_im = jnp.zeros((W, W), f32)
+            for i, p in enumerate(places):
+                base = i * 2 * W + m * W
+                back_re, back_im = back[base : base + W, :W], back[base : base + W, W:]
+                win_re, win_im = windows[i]
+                sum_re += win_re * back_re + win_im * back_im
+                sum_im += win_re * back_im - win_im * back_re
+            probe_grad_ref[2 * m] += sum_re
+            probe_grad_ref[2 * m + 1] += sum_im
+        for i, p in enumerate(places):
+            grads = [jnp.zeros((W, W), f32)] * 2
+            for m in range(MODES):
+                base = i * 2 * W + m * W
+                back_re, back_im = back[base : base + W, :W], back[base : base + W, W:]
+                probe_re, probe_im = probe_ref[2 * m], probe_ref[2 * m + 1]
+                grads[0] += probe_re * back_re + probe_im * back_im
+                grads[1] += probe_re * back_im - probe_im * back_re
+            top, left = offsets_ref[2 * p], offsets_ref[2 * p + 1]
+            for part, grad in enumerate(grads):
+                turned = pltpu.roll(grad, left, 1)
+                inside = jnp.where(lanes >= left, turned, 0.0)
+                object_grad_ref[part, pl.ds(top, W), :] += inside
+                object_grad_ref[2 + part, pl.ds(top, W), :] += turned - inside
         return carried
 
-    lax.fori_loop(0, POSITIONS, one, 0)
+    for copy in far_copies:
+        copy.wait()
+    lax.fori_loop(0, POSITIONS // GROUP, some, 0)
     probe_power = (
         probe_ref[0] ** 2 + probe_ref[1] ** 2 + probe_ref[2] ** 2 + probe_ref[3] ** 2
     )
@@ -281,6 +338,7 @@
 
 SMEM = pl.BlockSpec(memory_space=pltpu.SMEM)
 VMEM = pl.BlockSpec(memory_space=pltpu.VMEM)
+HBM = pl.BlockSpec(memory_space=pltpu.HBM)
 
 
 def params(mib):
@@ -294,7 +352,7 @@
     patterns = patterns.reshape(POSITIONS, W, W)
     offsets = offsets.reshape(2 * POSITIONS)
     probe_flat = probe.reshape(2 * MODES, W, W)
-    right_fwd, left_fwd, right_inv, left_inv = (jnp.asarray(t) for t in dft_tables())
+    tables = jnp.asarray(dft_tables())
     shifts = jnp.asarray(shift_tables())
 
     above = lax.ppermute(object_field[:, TILE - HALF :, :], "srow", shifted_to("srow", 1))
@@ -302,38 +360,40 @@
 
     sums = pl.pallas_call(
         lambda *refs: sums_kernel(row_dev, col_dev, *refs),
-        out_shape=jax.ShapeDtypeStruct((row_dev, W), f32),
+        out_shape=jax.ShapeDtypeStruct((row_dev * col_dev, W), f32),
         in_specs=[SMEM, VMEM],
         out_specs=VMEM,
         scratch_shapes=[pltpu.VMEM((POSITIONS, W), f32), pltpu.VMEM((POSITIONS, W), f32)],
         compiler_params=params(8),
         name="sums",
     )(place, patterns)
-    sums = spread(sums, "srow")
+    above, below, sums = lax.optimization_barrier((above, below, sums))
+    sums = spread(sums, ("srow", "scol"))
 
     tall = jnp.concatenate([above, object_field, below], axis=1)
     left_rim = lax.ppermute(tall[:, :, TILE - HALF :], "scol", shifted_to("scol", 1))
     right_rim = lax.ppermute(tall[:, :, :HALF], "scol", shifted_to("scol", -1))
-
-    sums = jnp.broadcast_to(jnp.sum(sums, axis=0, keepdims=True), (col_dev, W))
-    sums = spread(sums, "scol")
 
     near = jnp.concatenate([left_rim, tall[:, :, :HALF]], axis=2)
     blank = jnp.zeros((2, EXT, 2 * W - EXT), f32)
     far = jnp.concatenate([tall[:, :, HALF:], right_rim, blank], axis=2)
     ext = jnp.concatenate([near, far], axis=0)
 
-    far, windows = pl.pallas_call(
+    big = [pltpu.VMEM((6 * W, 2 * W), bf16), pltpu.VMEM((2 * W, 6 * W), bf16)]
+    far = pl.pallas_call(
         forward_kernel,
-        out_shape=(
-            jax.ShapeDtypeStruct((POSITIONS, 2 * W, 2 * W), f32),
-            jax.ShapeDtypeStruct((POSITIONS, 2, W, W), f32),
-        ),
-        in_specs=[SMEM, VMEM, VMEM, VMEM, VMEM],
-        out_specs=(VMEM, VMEM),
-        compiler_params=params(24),
+        out_shape=jax.ShapeDtypeStruct((POSITIONS, 2 * W, 2 * W), f32),
+        in_specs=[SMEM, VMEM, VMEM, VMEM],
+        out_specs=HBM,
+        scratch_shapes=big
+        + [
+            pltpu.VMEM((POSITIONS, 2 * W, 2 * W), f32),
+            pltpu.SemaphoreType.DMA((POSITIONS // GROUP,)),
+        ],
+        compiler_params=params(58),
+        cost_estimate=pl.CostEstimate(flops=6 << 30, bytes_accessed=7 << 20, transcendentals=0),
         name="forward",
-    )(offsets, ext, probe_flat, right_fwd, left_fwd)
+    )(offsets, ext, probe_flat, tables)
 
     ext_grad, probe_grad = pl.pallas_call(
         lambda *refs: backward_kernel(row_dev, col_dev, *refs),
@@ -341,12 +401,23 @@
             jax.ShapeDtypeStruct((4, EXT, W), f32),
             jax.ShapeDtypeStruct((2 * MODES, W, W), f32),
         ),
-        in_specs=[SMEM, SMEM] + [VMEM] * 8,
+        in_specs=[SMEM, SMEM, VMEM, VMEM, HBM, VMEM, VMEM, VMEM, VMEM],
         out_specs=(VMEM, VMEM),
-        scratch_shapes=[pltpu.VMEM((POSITIONS, W), f32)] * 3,
-        compiler_params=params(24),
+        scratch_shapes=[
+            pltpu.VMEM((POSITIONS, 8, W), f32),
+            pltpu.VMEM((POSITIONS, 8, W), f32),
+            pltpu.VMEM((POSITIONS, W), f32),
+        ]
+        + big
+        + [
+            pltpu.VMEM((POSITIONS, W, W), f32),
+            pltpu.VMEM((POSITIONS, 2 * W, 2 * W), f32),
+            pltpu.SemaphoreType.DMA((POSITIONS // GROUP,)),
+        ],
+        compiler_params=params(58),
+        cost_estimate=pl.CostEstimate(flops=8 << 30, bytes_accessed=9 << 20, transcendentals=0),
         name="backward",
-    )(offsets, place, sums, patterns, far, windows, probe_flat, shifts, right_inv, left_inv)
+    )(offsets, place, sums, patterns, far, ext, probe_flat, shifts, tables)
 
     from_below = lax.ppermute(ext_grad[:, :HALF, :], "srow", shifted_to("srow", -1))
     from_above = lax.ppermute(ext_grad[:, HALF + TILE :, :], "srow", shifted_to("srow", 1))

time: 130 us -> 107 us (0.82)
  local copies, waits for them, and re-layouts: 17 us -> 7.97 us
  waiting for transfers between devices: 29.9 us -> 21.3 us
  Pallas kernels: 30.9 us -> 22.9 us
  starting transfers between devices: 47.2 us -> 50.3 us
    pallas_call x1, Pallas kernels: 21.2 us -> 12 us  [on_device(): pl.pallas_call(lambda *refs: backward_kernel(row_dev, col_dev, *refs), ou...]
    unnamed x29 -> x13, local copies, waits for them, and re-layouts: 12.5 us -> 3.58 us
    ppermute x1, waiting for transfers between devices: 3.67 us -> 0.01 us  [on_device(): lax.ppermute(object_field[:, :HALF, :], 'srow', shifted_to('srow', -1))]
    all_to_all x5 -> x4, waiting for transfers between devices: 24.9 us -> 21.3 us  [spread(): return lax.all_to_all(values, axis, 0, 0, tiled=True)]
    ppermute x1, starting transfers between devices: 0.01 us -> 3.32 us  [on_device(): lax.ppermute(object_field[:, :HALF, :], 'srow', shifted_to('srow', -1))]
    ppermute x1, starting transfers between devices: 4.38 us -> 1.15 us  [on_device(): lax.ppermute(object_field[:, TILE - HALF:, :], 'srow', shifted_to('srow',...]
    all_to_all x5 -> x4, starting transfers between devices: 30.6 us -> 32.5 us  [spread(): return lax.all_to_all(values, axis, 0, 0, tiled=True)]
    ppermute x1, waiting for transfers between devices: 1.33 us -> 0.01 us  [on_device(): lax.ppermute(object_field[:, TILE - HALF:, :], 'srow', shifted_to('srow',...]
  transfers between devices with their start and end apart: 13 -> 12, of which waited for: 6 -> 4; matrix products, arithmetic and copies ran while one was open for 6% -> 6% of each run, Pallas kernels for 8% -> 10%
where the time goes in v2:
time: 107 us
  starting transfers between devices  50.3 us (47%)
  Pallas kernels  22.9 us (21%)
  waiting for transfers between devices  21.3 us (20%)
  local copies, waits for them, and re-layouts  7.97 us (7%)
  other arithmetic  3.48 us (3%)
    all_to_all x4, starting transfers between devices, spread(): return lax.all_to_all(values, axis, 0, 0, tiled=True)  32.5 us
    all_to_all x4, waiting for transfers between devices, spread(): return lax.all_to_all(values, axis, 0, 0, tiled=True)  21.3 us
    pallas_call x1, Pallas kernels, on_device(): pl.pallas_call(lambda *refs: backward_kernel(row_dev, col_dev, *refs), ou...  12 us
    pallas_call x1, Pallas kernels, on_device(): pl.pallas_call(forward_kernel, out_shape=jax.ShapeDtypeStruct((POSITIONS,...  9.45 us
    ppermute x1, starting transfers between devices, on_device(): right_rim = lax.ppermute(tall[:, :, :HALF], 'scol', shifted_to('scol', -1))  5.38 us
    unnamed x13, local copies, waits for them, and re-layouts  3.58 us
    ppermute x1, starting transfers between devices, on_device(): lax.ppermute(grad[:2, :, :HALF], 'scol', shifted_to('scol', -1))  3.55 us
    ppermute x1, starting transfers between devices, on_device(): lax.ppermute(object_field[:, :HALF, :], 'srow', shifted_to('srow', -1))  3.32 us
  transfers between devices with their start and end apart: 12, of which 4 were waited for; matrix products, arithmetic and copies ran while one was open for 6% of the time, Pallas kernels for 10%

profile of v2, /device:TPU:1, one launch (start us, length us, event | category | flops | bytes accessed | tf_op | source)
XLA Modules:
  0.0 106.8 jit_solution(12706102980984155022)
XLA Ops:
  0.6 0.9 fusion.5
  1.6 3.3 %collective-permute-start.1 = (f32[2,64,72]{2,1,0:T(8,128)S(1)}, f32[2,64,72]{2,1,0:T(8,128)S(1)}, u32[]{:S(2)}, u32[]{:S(2)}) collective-permute-start(f32[2,64,72]{2,1,0:T(8,128)S(1)} %get-tuple-element.19), channel_id=1, source_target_pairs={{0,240},{16,0},{32,16},{48,32},{64,48},{80,64},{96,80},{112,96},{1... | collective-permute-start | bytes 110600 | tf_op jit(solution)/shard_map/ppermute | solution.py:359
  4.9 1.2 %collective-permute-start = (f32[2,64,72]{2,1,0:T(8,128)S(1)}, f32[2,64,72]{2,1,0:T(8,128)S(1)}, u32[]{:S(2)}, u32[]{:S(2)}) collective-permute-start(f32[2,64,72]{2,1,0:T(8,128)S(1)} %get-tuple-element.20), channel_id=1, source_target_pairs={{0,16},{16,32},{32,48},{48,64},{64,80},{80,96},{96,112},{112,128},... | collective-permute-start | bytes 110600 | tf_op jit(solution)/shard_map/ppermute | solution.py:358
  6.1 1.2 %copy-done = f32[4,4,128,128]{3,2,1,0:T(8,128)S(1)} copy-done((f32[4,4,128,128]{3,2,1,0:T(8,128)S(1)}, f32[4,4,128,128]{3,2,1,0:T(8,128)}, u32[]{:S(2)}) %copy-start) | copy-done | bytes 1048600
  7.3 1.4 %sums.1 = f32[256,128]{1,0:T(8,128)} custom-call(s32[2]{0:T(128)S(1)} %pad_add_fusion.1.refs_0_.refs_1_, f32[16,128,128]{2,1,0:T(8,128)S(1)} %bitcast.11), custom_call_target="tpu_custom_call" | custom-call | tf_op jit(solution)/shard_map/sums/pallas_call | solution.py:361
  8.8 0.9 constant_dynamic-update-slice_fusion.1
  9.8 1.1 collective-permute-start.2
  10.9 5.4 %collective-permute-start.3 = (f32[2,200,64]{2,1,0:T(8,128)S(1)}, f32[2,200,64]{2,1,0:T(8,128)S(1)}, u32[]{:S(2)}, u32[]{:S(2)}) collective-permute-start(f32[2,200,64]{2,1,0:T(8,128)S(1)} %get-tuple-element.15), channel_id=1, source_target_pairs={{0,15},{1,0},{2,1},{3,2},{4,3},{5,4},{6,5},{7,6},{8,7},{9,8},{10,9... | collective-permute-start | bytes 307208 | tf_op jit(solution)/shard_map/ppermute | solution.py:375
  16.3 0.8 copy.12
  17.9 13.3 %all-to-all-start = ((f32[256,1,128]{2,1,0:T(1,128)}), f32[256,1,128]{2,1,0:T(1,128)S(1)}, u32[]{:S(2)}, u32[]{:S(2)}) async-start(f32[256,1,128]{2,1,0:T(1,128)} %bitcast.4), calls=%async_computation | async-start | bytes 262144 | tf_op jit(solution)/shard_map/all_to_all | solution.py:336
  31.2 0.9 maximum_maximum_fusion.ext_ref.refs_5_
  32.1 9.4 %forward.1.refs_4_ = f32[16,256,256]{2,1,0:T(8,128)} custom-call(s32[32]{0:T(128)} %reshape.23.offsets_ref.refs_0_, f32[4,200,128]{2,1,0:T(8,128)} %maximum_maximum_fusion.ext_ref.refs_5_, f32[4,128,128]{2,1,0:T(8,128)} %bitcast.13, bf16[4,128,128]{2,1,0:T(8,128)(2,1)} %constant.18.clone.tables_ref.refs_8_), custom_call_target="tpu_custom_call" | custom-call | flops 6442450944 | bytes 7340032 | tf_op jit(solution)/shard_map/forward/pallas_call | solution.py:383
  41.6 2.3 %all-to-all-done = f32[256,1,128]{2,1,0:T(1,128)S(1)} async-done(((f32[256,1,128]{2,1,0:T(1,128)}), f32[256,1,128]{2,1,0:T(1,128)S(1)}, u32[]{:S(2)}, u32[]{:S(2)}) %all-to-all-start) | async-done | bytes 131104 | tf_op jit(solution)/shard_map/all_to_all | solution.py:336
  44.5 12.0 %backward.1 = (f32[4,200,128]{2,1,0:T(8,128)}, f32[4,128,128]{2,1,0:T(8,128)}) custom-call(s32[32]{0:T(128)} %reshape.23.offsets_ref.refs_0_, s32[2]{0:T(128)} %copy-done.1, f32[256,128]{1,0:T(8,128)} %bitcast.16, f32[16,128,128]{2,1,0:T(8,128)} %bitcast.10, f32[16,256,256]{2,1,0:T(8,128)} %forward.1.refs_4_, ...), custom_call_target="tpu_custom_call" | custom-call | flops 8589934592 | bytes 9437184 | tf_op jit(solution)/shard_map/backward/pallas_call | solution.py:398
  56.6 5.2 %all-to-all-start.1 = ((f32[16,32,128]{2,1,0:T(8,128)}), f32[16,32,128]{2,1,0:T(8,128)S(1)}, u32[]{:S(2)}, u32[]{:S(2)}) async-start(f32[16,32,128]{2,1,0:T(8,128)} %bitcast.15), calls=%async_computation.1 | async-start | bytes 524288 | tf_op jit(solution)/shard_map/all_to_all | solution.py:336
  61.8 1.0 fusion.2
  63.0 3.1 %collective-permute-start.5 = (f32[4,64,128]{2,1,0:T(8,128)S(1)}, f32[4,64,128]{2,1,0:T(8,128)S(1)}, u32[]{:S(2)}, u32[]{:S(2)}) collective-permute-start(f32[4,64,128]{2,1,0:T(8,128)S(1)} %get-tuple-element.13), channel_id=1, source_target_pairs={{0,16},{16,32},{32,48},{48,64},{64,80},{80,96},{96,112},{112,128},... | collective-permute-start | bytes 393224 | tf_op jit(solution)/shard_map/ppermute | solution.py:423
  66.1 4.6 %all-to-all-done.1 = f32[16,32,128]{2,1,0:T(8,128)S(1)} async-done(((f32[16,32,128]{2,1,0:T(8,128)}), f32[16,32,128]{2,1,0:T(8,128)S(1)}, u32[]{:S(2)}, u32[]{:S(2)}) %all-to-all-start.1) | async-done | bytes 262176 | tf_op jit(solution)/shard_map/all_to_all | solution.py:336
  71.4 7.6 %all-to-all-start.2 = ((f32[16,32,128]{2,1,0:T(8,128)}), f32[16,32,128]{2,1,0:T(8,128)S(1)}, u32[]{:S(2)}, u32[]{:S(2)}) async-start(f32[16,32,128]{2,1,0:T(8,128)} %broadcast_in_dim.7), calls=%async_computation.2 | async-start | bytes 524288 | tf_op jit(solution)/shard_map/all_to_all | solution.py:336
  79.1 0.9 pad_add_fusion
  80.1 3.6 %collective-permute-start.6 = (f32[2,72,64]{2,1,0:T(8,128)S(1)}, f32[2,72,64]{2,1,0:T(8,128)S(1)}, u32[]{:S(2)}, u32[]{:S(2)}) collective-permute-start(f32[2,72,64]{2,1,0:T(8,128)S(1)} %get-tuple-element.16), channel_id=1, source_target_pairs={{0,15},{1,0},{2,1},{3,2},{4,3},{5,4},{6,5},{7,6},{8,7},{9,8},{10,9... | collective-permute-start | bytes 110600 | tf_op jit(solution)/shard_map/ppermute | solution.py:431
  83.7 6.3 %all-to-all-done.2 = f32[16,32,128]{2,1,0:T(8,128)S(1)} async-done(((f32[16,32,128]{2,1,0:T(8,128)}), f32[16,32,128]{2,1,0:T(8,128)S(1)}, u32[]{:S(2)}, u32[]{:S(2)}) %all-to-all-start.2) | async-done | bytes 262176 | tf_op jit(solution)/shard_map/all_to_all | solution.py:336
  90.7 6.4 %all-to-all-start.3 = ((f32[16,32,128]{2,1,0:T(8,128)}), f32[16,32,128]{2,1,0:T(8,128)S(1)}, u32[]{:S(2)}, u32[]{:S(2)}) async-start(f32[16,32,128]{2,1,0:T(8,128)} %broadcast_in_dim.8), calls=%async_computation.3 | async-start | bytes 524288 | tf_op jit(solution)/shard_map/all_to_all | solution.py:336
  98.0 8.1 %all-to-all-done.3 = f32[16,32,128]{2,1,0:T(8,128)S(1)} async-done(((f32[16,32,128]{2,1,0:T(8,128)}), f32[16,32,128]{2,1,0:T(8,128)S(1)}, u32[]{:S(2)}, u32[]{:S(2)}) %all-to-all-start.3) | async-done | bytes 262176 | tf_op jit(solution)/shard_map/all_to_all | solution.py:336
  (36 shorter events, 5.0 us)
Async XLA Ops:
  1.6 7.2 %collective-permute-start.1 = (f32[2,64,72]{2,1,0:T(8,128)S(1)}, f32[2,64,72]{2,1,0:T(8,128)S(1)}, u32[]{:S(2)}, u32[]{:S(2)}) collective-permute-start(f32[2,64,72]{2,1,0:T(8,128)S(1)} %get-tuple-element.19), channel_id=1, source_target_pairs={{0,240},{16,0},{32,16},{48,32},{64,48},{80,64},{96,80},{112,96},{1... | collective-permute-start | bytes 110600 | tf_op jit(solution)/shard_map/ppermute | solution.py:359
  4.9 3.9 %collective-permute-start = (f32[2,64,72]{2,1,0:T(8,128)S(1)}, f32[2,64,72]{2,1,0:T(8,128)S(1)}, u32[]{:S(2)}, u32[]{:S(2)}) collective-permute-start(f32[2,64,72]{2,1,0:T(8,128)S(1)} %get-tuple-element.20), channel_id=1, source_target_pairs={{0,16},{16,32},{32,48},{48,64},{64,80},{80,96},{96,112},{112,128},... | collective-permute-start | bytes 110600 | tf_op jit(solution)/shard_map/ppermute | solution.py:358
  6.1 35.5 %copy-start.1 = (s32[2]{0:T(128)}, s32[2]{0:T(128)S(1)}, u32[]{:S(2)}) copy-start(s32[2]{0:T(128)S(1)} %pad_add_fusion.1.refs_0_.refs_1_) | copy-start | bytes 28
  6.1 1.2 %copy-start = (f32[4,4,128,128]{3,2,1,0:T(8,128)S(1)}, f32[4,4,128,128]{3,2,1,0:T(8,128)}, u32[]{:S(2)}) copy-start(f32[4,4,128,128]{3,2,1,0:T(8,128)} %param.6) | copy-start | bytes 3145732
  9.8 21.4 %collective-permute-start.2 = (f32[2,200,64]{2,1,0:T(8,128)S(1)}, f32[2,200,64]{2,1,0:T(8,128)S(1)}, u32[]{:S(2)}, u32[]{:S(2)}) collective-permute-start(f32[2,200,64]{2,1,0:T(8,128)S(1)} %get-tuple-element.14), channel_id=1, source_target_pairs={{0,1},{1,2},{2,3},{3,4},{4,5},{5,6},{6,7},{7,8},{8,9},{9,10},{10,1... | collective-permute-start | bytes 307208 | tf_op jit(solution)/shard_map/ppermute | solution.py:374
  10.9 20.3 %collective-permute-start.3 = (f32[2,200,64]{2,1,0:T(8,128)S(1)}, f32[2,200,64]{2,1,0:T(8,128)S(1)}, u32[]{:S(2)}, u32[]{:S(2)}) collective-permute-start(f32[2,200,64]{2,1,0:T(8,128)S(1)} %get-tuple-element.15), channel_id=1, source_target_pairs={{0,15},{1,0},{2,1},{3,2},{4,3},{5,4},{6,5},{7,6},{8,7},{9,8},{10,9... | collective-permute-start | bytes 307208 | tf_op jit(solution)/shard_map/ppermute | solution.py:375
  17.9 26.0 %all-to-all-start = ((f32[256,1,128]{2,1,0:T(1,128)}), f32[256,1,128]{2,1,0:T(1,128)S(1)}, u32[]{:S(2)}, u32[]{:S(2)}) async-start(f32[256,1,128]{2,1,0:T(1,128)} %bitcast.4), calls=%async_computation | async-start | bytes 262144 | tf_op jit(solution)/shard_map/all_to_all | solution.py:336
  43.9 0.7 copy-start.4
  56.6 40.6 %copy-start.2 = (f32[2,72,72]{2,1,0:T(8,128)S(1)}, f32[2,72,72]{2,1,0:T(8,128)}, u32[]{:S(2)}) copy-start(f32[2,72,72]{2,1,0:T(8,128)} %param.8) | copy-start | bytes 124420
  56.6 49.5 %copy-start.3 = (f32[2,2,128,128]{3,2,1,0:T(8,128)S(1)}, f32[2,2,128,128]{3,2,1,0:T(8,128)}, u32[]{:S(2)}) copy-start(f32[2,2,128,128]{3,2,1,0:T(8,128)} %param.9) | copy-start | bytes 786436
  56.6 14.1 %all-to-all-start.1 = ((f32[16,32,128]{2,1,0:T(8,128)}), f32[16,32,128]{2,1,0:T(8,128)S(1)}, u32[]{:S(2)}, u32[]{:S(2)}) async-start(f32[16,32,128]{2,1,0:T(8,128)} %bitcast.15), calls=%async_computation.1 | async-start | bytes 524288 | tf_op jit(solution)/shard_map/all_to_all | solution.py:336
  62.8 16.3 %collective-permute-start.4 = (f32[4,64,128]{2,1,0:T(8,128)S(1)}, f32[4,64,128]{2,1,0:T(8,128)S(1)}, u32[]{:S(2)}, u32[]{:S(2)}) collective-permute-start(f32[4,64,128]{2,1,0:T(8,128)S(1)} %get-tuple-element.12), channel_id=1, source_target_pairs={{0,240},{16,0},{32,16},{48,32},{64,48},{80,64},{96,80},{112,96},{1... | collective-permute-start | bytes 393224 | tf_op jit(solution)/shard_map/ppermute | solution.py:422
  63.0 16.1 %collective-permute-start.5 = (f32[4,64,128]{2,1,0:T(8,128)S(1)}, f32[4,64,128]{2,1,0:T(8,128)S(1)}, u32[]{:S(2)}, u32[]{:S(2)}) collective-permute-start(f32[4,64,128]{2,1,0:T(8,128)S(1)} %get-tuple-element.13), channel_id=1, source_target_pairs={{0,16},{16,32},{32,48},{48,64},{64,80},{80,96},{96,112},{112,128},... | collective-permute-start | bytes 393224 | tf_op jit(solution)/shard_map/ppermute | solution.py:423
  71.4 18.5 %all-to-all-start.2 = ((f32[16,32,128]{2,1,0:T(8,128)}), f32[16,32,128]{2,1,0:T(8,128)S(1)}, u32[]{:S(2)}, u32[]{:S(2)}) async-start(f32[16,32,128]{2,1,0:T(8,128)} %broadcast_in_dim.7), calls=%async_computation.2 | async-start | bytes 524288 | tf_op jit(solution)/shard_map/all_to_all | solution.py:336
  80.1 17.1 %collective-permute-start.6 = (f32[2,72,64]{2,1,0:T(8,128)S(1)}, f32[2,72,64]{2,1,0:T(8,128)S(1)}, u32[]{:S(2)}, u32[]{:S(2)}) collective-permute-start(f32[2,72,64]{2,1,0:T(8,128)S(1)} %get-tuple-element.16), channel_id=1, source_target_pairs={{0,15},{1,0},{2,1},{3,2},{4,3},{5,4},{6,5},{7,6},{8,7},{9,8},{10,9... | collective-permute-start | bytes 110600 | tf_op jit(solution)/shard_map/ppermute | solution.py:431
  83.6 13.5 %collective-permute-start.7 = (f32[2,72,64]{2,1,0:T(8,128)S(1)}, f32[2,72,64]{2,1,0:T(8,128)S(1)}, u32[]{:S(2)}, u32[]{:S(2)}) collective-permute-start(f32[2,72,64]{2,1,0:T(8,128)S(1)} %get-tuple-element.17), channel_id=1, source_target_pairs={{0,1},{1,2},{2,3},{3,4},{4,5},{5,6},{6,7},{7,8},{8,9},{9,10},{10,1... | collective-permute-start | bytes 110600 | tf_op jit(solution)/shard_map/ppermute | solution.py:432
  90.7 15.3 %all-to-all-start.3 = ((f32[16,32,128]{2,1,0:T(8,128)}), f32[16,32,128]{2,1,0:T(8,128)S(1)}, u32[]{:S(2)}, u32[]{:S(2)}) async-start(f32[16,32,128]{2,1,0:T(8,128)} %broadcast_in_dim.8), calls=%async_computation.3 | async-start | bytes 524288 | tf_op jit(solution)/shard_map/all_to_all | solution.py:336

commit v3 on v2

--- a/solution.py
+++ b/solution.py
@@ -17,7 +17,7 @@
 POSITIONS = PR * PC
 TILE = 72
 EXT = TILE + W
-GROUP = 4
+GROUP = 8
 AHEAD = 8
 
 obj_rate = 0.2
@@ -106,14 +106,14 @@
     return lax.broadcasted_iota(jnp.int32, shape, len(shape) - 2)
 
 
-def place_of(place_ref, row_dev, col_dev, shape):
+def place_of(scalars_ref, row_dev, col_dev, shape):
     position = row_iota(shape)
-    row = (place_ref[0] * PR + position // PC).astype(f32)
-    col = (place_ref[1] * PC + position % PC).astype(f32)
+    row = (scalars_ref[2 * POSITIONS] * PR + position // PC).astype(f32)
+    col = (scalars_ref[2 * POSITIONS + 1] * PC + position % PC).astype(f32)
     return (row + 0.5) / (PR * row_dev) - 0.5, (col + 0.5) / (PC * col_dev) - 0.5
 
 
-def sums_kernel(row_dev, col_dev, place_ref, patterns_ref, out_ref, total_ref, tilt_ref):
+def sums_kernel(row_dev, col_dev, scalars_ref, patterns_ref, out_ref, total_ref, tilt_ref):
     k = row_iota((W, W))
     freq = (((k + HALF) % W) - HALF).astype(f32)
     for p in range(POSITIONS):
@@ -126,7 +126,7 @@
     weight = jnp.sum(total, axis=1, keepdims=True)
     tilt_row = jnp.sum(tilt_ref[...], axis=1, keepdims=True)
     tilt_col = jnp.sum(total * col_freq, axis=1, keepdims=True)
-    row, col = place_of(place_ref, row_dev, col_dev, (POSITIONS, W))
+    row, col = place_of(scalars_ref, row_dev, col_dev, (POSITIONS, W))
     terms = [
         weight,
         weight * row,
@@ -157,7 +157,7 @@
 
 
 def forward_kernel(
-    offsets_ref, ext_ref, probe_ref, tables_ref, far_out,
+    scalars_ref, ext_ref, probe_ref, tables_ref, far_out,
     right_ref, left_ref, far_ref, far_sem,
 ):
     fill_tables(tables_ref, right_ref, left_ref, False)
@@ -166,7 +166,7 @@
         places = [group * GROUP + i for i in range(GROUP)]
         waves = []
         for p in places:
-            row, col = offsets_ref[2 * p], offsets_ref[2 * p + 1]
+            row, col = scalars_ref[2 * p], scalars_ref[2 * p + 1]
             win_re = cut_window(ext_ref, 0, row, col)
             win_im = cut_window(ext_ref, 1, row, col)
             for m in range(MODES):
@@ -223,7 +223,7 @@
 
 
 def backward_kernel(
-    row_dev, col_dev, offsets_ref, place_ref, sums_ref, patterns_ref, far_in, ext_ref, probe_ref,
+    row_dev, col_dev, scalars_ref, sums_ref, patterns_ref, far_in, ext_ref, probe_ref,
     shift_ref, tables_ref, object_grad_ref, probe_grad_ref,
     cols_ref, rows_ref, nyquist_ref, right_ref, left_ref, target_ref, far_ref, far_sem,
 ):
@@ -235,7 +235,7 @@
         copy.start()
 
     sums = jnp.sum(sums_ref[...], axis=0, keepdims=True)
-    row, col = place_of(place_ref, row_dev, col_dev, (POSITIONS, W))
+    row, col = place_of(scalars_ref, row_dev, col_dev, (POSITIONS, W))
     shift_row, shift_col = descan_of(sums, row, col)
     lane = lane_iota((POSITIONS, W))
     freq = jnp.where(lane <= HALF, lane, lane - HALF).astype(f32)
@@ -288,7 +288,7 @@
         lanes = lane_iota((W, W))
         windows = []
         for p in places:
-            at = offsets_ref[2 * p], offsets_ref[2 * p + 1]
+            at = scalars_ref[2 * p], scalars_ref[2 * p + 1]
             windows.append((cut_window(ext_ref, 0, *at), cut_window(ext_ref, 1, *at)))
         for m in range(MODES):
             sum_re = jnp.zeros((W, W), f32)
@@ -309,7 +309,7 @@
                 probe_re, probe_im = probe_ref[2 * m], probe_ref[2 * m + 1]
                 grads[0] += probe_re * back_re + probe_im * back_im
                 grads[1] += probe_re * back_im - probe_im * back_re
-            top, left = offsets_ref[2 * p], offsets_ref[2 * p + 1]
+            top, left = scalars_ref[2 * p], scalars_ref[2 * p + 1]
             for part, grad in enumerate(grads):
                 turned = pltpu.roll(grad, left, 1)
                 inside = jnp.where(lanes >= left, turned, 0.0)
@@ -332,8 +332,20 @@
     return [(i, (i + step) % count) for i in range(count)]
 
 
-def spread(values, axis):
-    return lax.all_to_all(values, axis, 0, 0, tiled=True)
+def spread(values, groups=None):
+    return lax.all_to_all(
+        values, ("srow", "scol"), 0, 0, axis_index_groups=groups, tiled=True
+    )
+
+
+def two_levels(row_dev, col_dev):
+    near, across = [], []
+    for pair in range(col_dev // 2):
+        near.append([r * col_dev + 2 * pair + c for r in range(row_dev) for c in range(2)])
+    for r in range(row_dev):
+        for c in range(2):
+            across.append([r * col_dev + 2 * pair + c for pair in range(col_dev // 2)])
+    return near, across
 
 
 SMEM = pl.BlockSpec(memory_space=pltpu.SMEM)
@@ -349,8 +361,8 @@
     row_dev = lax.axis_size("srow")
     col_dev = lax.axis_size("scol")
     place = jnp.stack([lax.axis_index("srow"), lax.axis_index("scol")]).astype(jnp.int32)
+    scalars = jnp.concatenate([offsets.reshape(2 * POSITIONS), place])
     patterns = patterns.reshape(POSITIONS, W, W)
-    offsets = offsets.reshape(2 * POSITIONS)
     probe_flat = probe.reshape(2 * MODES, W, W)
     tables = jnp.asarray(dft_tables())
     shifts = jnp.asarray(shift_tables())
@@ -366,9 +378,9 @@
         scratch_shapes=[pltpu.VMEM((POSITIONS, W), f32), pltpu.VMEM((POSITIONS, W), f32)],
         compiler_params=params(8),
         name="sums",
-    )(place, patterns)
-    above, below, sums = lax.optimization_barrier((above, below, sums))
-    sums = spread(sums, ("srow", "scol"))
+    )(scalars, patterns)
+    above, below, _ = lax.optimization_barrier((above, below, sums))
+    sums = spread(sums.reshape(row_dev * col_dev, 1, W)).reshape(row_dev * col_dev, W)
 
     tall = jnp.concatenate([above, object_field, below], axis=1)
     left_rim = lax.ppermute(tall[:, :, TILE - HALF :], "scol", shifted_to("scol", 1))
@@ -391,9 +403,9 @@
             pltpu.SemaphoreType.DMA((POSITIONS // GROUP,)),
         ],
         compiler_params=params(58),
-        cost_estimate=pl.CostEstimate(flops=6 << 30, bytes_accessed=7 << 20, transcendentals=0),
+        cost_estimate=pl.CostEstimate(flops=0, bytes_accessed=0, transcendentals=0),
         name="forward",
-    )(offsets, ext, probe_flat, tables)
+    )(scalars, ext, probe_flat, tables)
 
     ext_grad, probe_grad = pl.pallas_call(
         lambda *refs: backward_kernel(row_dev, col_dev, *refs),
@@ -401,7 +413,7 @@
             jax.ShapeDtypeStruct((4, EXT, W), f32),
             jax.ShapeDtypeStruct((2 * MODES, W, W), f32),
         ),
-        in_specs=[SMEM, SMEM, VMEM, VMEM, HBM, VMEM, VMEM, VMEM, VMEM],
+        in_specs=[SMEM, VMEM, VMEM, HBM, VMEM, VMEM, VMEM, VMEM],
         out_specs=(VMEM, VMEM),
         scratch_shapes=[
             pltpu.VMEM((POSITIONS, 8, W), f32),
@@ -414,16 +426,19 @@
             pltpu.VMEM((POSITIONS, 2 * W, 2 * W), f32),
             pltpu.SemaphoreType.DMA((POSITIONS // GROUP,)),
         ],
-        compiler_params=params(58),
+        compiler_params=params(50),
         cost_estimate=pl.CostEstimate(flops=8 << 30, bytes_accessed=9 << 20, transcendentals=0),
         name="backward",
-    )(offsets, place, sums, patterns, far, ext, probe_flat, shifts, tables)
+    )(scalars, sums, patterns, far, ext, probe_flat, shifts, tables)
 
     from_below = lax.ppermute(ext_grad[:, :HALF, :], "srow", shifted_to("srow", -1))
     from_above = lax.ppermute(ext_grad[:, HALF + TILE :, :], "srow", shifted_to("srow", 1))
 
-    chunk = 2 * MODES * W // row_dev
-    parts = spread(probe_grad.reshape(row_dev, chunk, W), "srow")
+    near, across = two_levels(row_dev, col_dev)
+    count = len(near[0])
+    chunk = 2 * MODES * W // count
+    part = jnp.sum(spread(probe_grad.reshape(count, chunk, W), near), axis=0)
+    from_below, from_above, _ = lax.optimization_barrier((from_below, from_above, part))
 
     grad = ext_grad[:, HALF : HALF + TILE, :]
     grad = grad + jnp.pad(from_below, ((0, 0), (TILE - HALF, 0), (0, 0)))
@@ -433,10 +448,9 @@
         grad[2:, :, TILE - HALF : TILE], "scol", shifted_to("scol", 1)
     )
 
-    part = jnp.sum(parts, axis=0)
-    part = spread(jnp.broadcast_to(part[None], (col_dev, chunk, W)), "scol")
-    part = jnp.sum(part, axis=0)
-    total = spread(jnp.broadcast_to(part[None], (row_dev, chunk, W)), "srow")
+    part = jnp.sum(spread(jnp.broadcast_to(part[None], (len(across[0]), chunk, W)), across), axis=0)
+    from_right, from_left, _ = lax.optimization_barrier((from_right, from_left, part))
+    total = spread(jnp.broadcast_to(part[None], (count, chunk, W)), near)
 
     grad = jnp.concatenate([grad[:2, :, HALF:], grad[2:, :, : TILE - HALF]], axis=2)
     grad = grad + jnp.pad(from_right, ((0, 0), (0, 0), (TILE - HALF, 0)))

time: 107 us -> 101 us (0.944)
  Pallas kernels: 22.9 us -> 21 us
  waiting for transfers between devices: 21.3 us -> 19.7 us
  local copies, waits for them, and re-layouts: 7.97 us -> 6.51 us
    all_to_all x4, waiting for transfers between devices: 21.3 us -> 19.7 us  [spread(): lax.all_to_all(values, ('srow', 'scol'), 0, 0, axis_index_groups=groups,...]
    pallas_call x1, Pallas kernels: 12 us -> 10.6 us  [on_device(): pl.pallas_call(lambda *refs: backward_kernel(row_dev, col_dev, *refs), ou...]
    unnamed x13 -> x21, local copies, waits for them, and re-layouts: 3.58 us -> 3.71 us
  transfers between devices with their start and end apart: 12 -> 12, of which waited for: 4 -> 4; matrix products, arithmetic and copies ran while one was open for 6% -> 4% of each run, Pallas kernels for 10% -> 10%
where the time goes in v3:
time: 101 us; the launch traced here: 100 us
  starting transfers between devices  49.4 us (49%)
  Pallas kernels  21 us (21%)
  waiting for transfers between devices  19.7 us (20%)
  local copies, waits for them, and re-layouts  6.51 us (6%)
  other arithmetic  2.59 us (3%)
    all_to_all x4, starting transfers between devices, spread(): lax.all_to_all(values, ('srow', 'scol'), 0, 0, axis_index_groups=groups,...  31.6 us
    all_to_all x4, waiting for transfers between devices, spread(): lax.all_to_all(values, ('srow', 'scol'), 0, 0, axis_index_groups=groups,...  19.7 us
    pallas_call x1, Pallas kernels, on_device(): pl.pallas_call(lambda *refs: backward_kernel(row_dev, col_dev, *refs), ou...  10.6 us
    pallas_call x1, Pallas kernels, on_device(): pl.pallas_call(forward_kernel, out_shape=jax.ShapeDtypeStruct((POSITIONS,...  8.96 us
    ppermute x1, starting transfers between devices, on_device(): right_rim = lax.ppermute(tall[:, :, :HALF], 'scol', shifted_to('scol', -1))  5.38 us
    unnamed x21, local copies, waits for them, and re-layouts  3.71 us
    ppermute x1, starting transfers between devices, on_device(): lax.ppermute(grad[:2, :, :HALF], 'scol', shifted_to('scol', -1))  3.56 us
    ppermute x1, starting transfers between devices, on_device(): lax.ppermute(object_field[:, :HALF, :], 'srow', shifted_to('srow', -1))  3.32 us
  transfers between devices with their start and end apart: 12, of which 4 were waited for; matrix products, arithmetic and copies ran while one was open for 4% of the time, Pallas kernels for 10%

profile of v3, /device:TPU:1, one launch (start us, length us, event | category | flops | bytes accessed | tf_op | source)
XLA Modules:
  0.0 100.1 jit_solution(17050703297229519258)
XLA Ops:
  0.6 0.9 fusion.5
  1.6 3.3 %collective-permute-start.1 = (f32[2,64,72]{2,1,0:T(8,128)S(1)}, f32[2,64,72]{2,1,0:T(8,128)S(1)}, u32[]{:S(2)}, u32[]{:S(2)}) collective-permute-start(f32[2,64,72]{2,1,0:T(8,128)S(1)} %get-tuple-element.25), channel_id=1, source_target_pairs={{0,240},{16,0},{32,16},{48,32},{64,48},{80,64},{96,80},{112,96},{1... | collective-permute-start | bytes 110600 | tf_op jit(solution)/shard_map/ppermute | solution.py:371
  4.9 1.2 %collective-permute-start = (f32[2,64,72]{2,1,0:T(8,128)S(1)}, f32[2,64,72]{2,1,0:T(8,128)S(1)}, u32[]{:S(2)}, u32[]{:S(2)}) collective-permute-start(f32[2,64,72]{2,1,0:T(8,128)S(1)} %get-tuple-element.26), channel_id=1, source_target_pairs={{0,16},{16,32},{32,48},{48,64},{64,80},{80,96},{96,112},{112,128},... | collective-permute-start | bytes 110600 | tf_op jit(solution)/shard_map/ppermute | solution.py:370
  6.0 0.8 copy.12
  7.0 1.2 %copy-done.2 = f32[4,4,128,128]{3,2,1,0:T(8,128)S(1)} copy-done((f32[4,4,128,128]{3,2,1,0:T(8,128)S(1)}, f32[4,4,128,128]{3,2,1,0:T(8,128)}, u32[]{:S(2)}) %copy-start.2) | copy-done | bytes 1048600
  8.2 1.4 %sums.1 = f32[256,128]{1,0:T(8,128)} custom-call(s32[34]{0:T(128)S(1)} %pad_add_fusion.1.refs_0_.scalars_ref, f32[16,128,128]{2,1,0:T(8,128)S(1)} %bitcast.12), custom_call_target="tpu_custom_call" | custom-call | tf_op jit(solution)/shard_map/sums/pallas_call | solution.py:373
  9.7 1.0 %constant_dynamic-update-slice_fusion.1 = f32[2,200,72]{2,1,0:T(8,128)S(1)} fusion(f32[2,200,72]{2,1,0:T(8,128)S(1)} %constant_dynamic-update-slice_fusion.2, f32[2,72,72]{2,1,0:T(8,128)} %param.8), kind=kLoop, calls=%fused_computation.7 | loop fusion | bytes 115200
  10.9 1.1 %collective-permute-start.2 = (f32[2,200,64]{2,1,0:T(8,128)S(1)}, f32[2,200,64]{2,1,0:T(8,128)S(1)}, u32[]{:S(2)}, u32[]{:S(2)}) collective-permute-start(f32[2,200,64]{2,1,0:T(8,128)S(1)} %get-tuple-element.20), channel_id=1, source_target_pairs={{0,1},{1,2},{2,3},{3,4},{4,5},{5,6},{6,7},{7,8},{8,9},{9,10},{10,1... | collective-permute-start | bytes 307208 | tf_op jit(solution)/shard_map/ppermute | solution.py:386
  11.9 5.4 %collective-permute-start.3 = (f32[2,200,64]{2,1,0:T(8,128)S(1)}, f32[2,200,64]{2,1,0:T(8,128)S(1)}, u32[]{:S(2)}, u32[]{:S(2)}) collective-permute-start(f32[2,200,64]{2,1,0:T(8,128)S(1)} %get-tuple-element.21), channel_id=1, source_target_pairs={{0,15},{1,0},{2,1},{3,2},{4,3},{5,4},{6,5},{7,6},{8,7},{9,8},{10,9... | collective-permute-start | bytes 307208 | tf_op jit(solution)/shard_map/ppermute | solution.py:387
  17.3 13.0 %all-to-all-start = ((f32[256,1,128]{2,1,0:T(1,128)}), f32[256,1,128]{2,1,0:T(1,128)S(1)}, u32[]{:S(2)}, u32[]{:S(2)}) async-start(f32[256,1,128]{2,1,0:T(1,128)} %bitcast.4), calls=%async_computation | async-start | bytes 262144 | tf_op jit(solution)/shard_map/all_to_all | solution.py:336
  30.5 0.9 maximum_maximum_fusion.ext_ref.refs_4_
  31.5 9.0 %forward.1.refs_3_ = f32[16,256,256]{2,1,0:T(8,128)} custom-call(s32[34]{0:T(128)} %copy-done.5, f32[4,200,128]{2,1,0:T(8,128)} %maximum_maximum_fusion.ext_ref.refs_4_, f32[4,128,128]{2,1,0:T(8,128)} %bitcast.10, bf16[4,128,128]{2,1,0:T(8,128)(2,1)} %constant.18.clone.tables_ref.refs_7_), custom_call_target="tpu_custom_call" | custom-call | tf_op jit(solution)/shard_map/forward/pallas_call | solution.py:395
  40.5 2.6 %all-to-all-done = f32[256,1,128]{2,1,0:T(1,128)S(1)} async-done(((f32[256,1,128]{2,1,0:T(1,128)}), f32[256,1,128]{2,1,0:T(1,128)S(1)}, u32[]{:S(2)}, u32[]{:S(2)}) %all-to-all-start) | async-done | bytes 131104 | tf_op jit(solution)/shard_map/all_to_all | solution.py:336
  43.7 10.6 %backward.1 = (f32[4,200,128]{2,1,0:T(8,128)S(1)}, f32[4,128,128]{2,1,0:T(8,128)}) custom-call(s32[34]{0:T(128)S(1)} %copy-done.6, f32[256,128]{1,0:T(8,128)S(1)} %bitcast.14, f32[16,128,128]{2,1,0:T(8,128)S(1)} %bitcast.13, f32[16,256,256]{2,1,0:T(8,128)} %forward.1.refs_3_, f32[4,200,128]{2,1,0:T(8,128)S(1)} %copy-done, f32[4,128,128]{2,1,0:T(8,128)S(1)} %bitcast.11, ...), custom_call_target="tpu_custom_call" | custom-call | flops 8589934592 | bytes 9437184 | tf_op jit(solution)/shard_map/backward/pallas_call | solution.py:410
  54.3 4.9 %all-to-all-start.1 = ((f32[32,16,128]{2,1,0:T(8,128)}), f32[32,16,128]{2,1,0:T(8,128)S(1)}, u32[]{:S(2)}, u32[]{:S(2)}) async-start(f32[32,16,128]{2,1,0:T(8,128)} %bitcast.7), calls=%async_computation.1 | async-start | bytes 524288 | tf_op jit(solution)/shard_map/all_to_all | solution.py:336
  59.3 3.2 %collective-permute-start.5 = (f32[4,64,128]{2,1,0:T(8,128)S(1)}, f32[4,64,128]{2,1,0:T(8,128)S(1)}, u32[]{:S(2)}, u32[]{:S(2)}) collective-permute-start(f32[4,64,128]{2,1,0:T(8,128)S(1)} %get-tuple-element.18), channel_id=1, source_target_pairs={{0,16},{16,32},{32,48},{48,64},{64,80},{80,96},{96,112},{112,128},... | collective-permute-start | bytes 393224 | tf_op jit(solution)/shard_map/ppermute | solution.py:435
  62.5 5.9 %all-to-all-done.1 = f32[32,16,128]{2,1,0:T(8,128)S(1)} async-done(((f32[32,16,128]{2,1,0:T(8,128)}), f32[32,16,128]{2,1,0:T(8,128)S(1)}, u32[]{:S(2)}, u32[]{:S(2)}) %all-to-all-start.1) | async-done | bytes 262176 | tf_op jit(solution)/shard_map/all_to_all | solution.py:336
  69.0 7.4 %all-to-all-start.2 = ((f32[8,16,128]{2,1,0:T(8,128)}), f32[8,16,128]{2,1,0:T(8,128)S(1)}, u32[]{:S(2)}, u32[]{:S(2)}) async-start(f32[8,16,128]{2,1,0:T(8,128)} %broadcast_in_dim.7), calls=%async_computation.2 | async-start | bytes 131072 | tf_op jit(solution)/shard_map/all_to_all | solution.py:336
  76.7 3.6 %collective-permute-start.6 = (f32[2,72,64]{2,1,0:T(8,128)S(1)}, f32[2,72,64]{2,1,0:T(8,128)S(1)}, u32[]{:S(2)}, u32[]{:S(2)}) collective-permute-start(f32[2,72,64]{2,1,0:T(8,128)S(1)} %get-tuple-element.23), channel_id=1, source_target_pairs={{0,15},{1,0},{2,1},{3,2},{4,3},{5,4},{6,5},{7,6},{8,7},{9,8},{10,9... | collective-permute-start | bytes 110600 | tf_op jit(solution)/shard_map/ppermute | solution.py:446
  80.3 3.4 %all-to-all-done.2 = f32[8,16,128]{2,1,0:T(8,128)S(1)} async-done(((f32[8,16,128]{2,1,0:T(8,128)}), f32[8,16,128]{2,1,0:T(8,128)S(1)}, u32[]{:S(2)}, u32[]{:S(2)}) %all-to-all-start.2) | async-done | bytes 65568 | tf_op jit(solution)/shard_map/all_to_all | solution.py:336
  84.4 6.3 %all-to-all-start.3 = ((f32[32,16,128]{2,1,0:T(8,128)}), f32[32,16,128]{2,1,0:T(8,128)S(1)}, u32[]{:S(2)}, u32[]{:S(2)}) async-start(f32[32,16,128]{2,1,0:T(8,128)} %broadcast_in_dim.8), calls=%async_computation.3 | async-start | bytes 524288 | tf_op jit(solution)/shard_map/all_to_all | solution.py:336
  90.7 0.7 fusion.1
  91.5 7.8 %all-to-all-done.3 = f32[32,16,128]{2,1,0:T(8,128)S(1)} async-done(((f32[32,16,128]{2,1,0:T(8,128)}), f32[32,16,128]{2,1,0:T(8,128)S(1)}, u32[]{:S(2)}, u32[]{:S(2)}) %all-to-all-start.3) | async-done | bytes 262176 | tf_op jit(solution)/shard_map/all_to_all | solution.py:336
  99.3 0.7 sub.7
  (44 shorter events, 2.8 us)
Async XLA Ops:
  1.6 8.1 %collective-permute-start.1 = (f32[2,64,72]{2,1,0:T(8,128)S(1)}, f32[2,64,72]{2,1,0:T(8,128)S(1)}, u32[]{:S(2)}, u32[]{:S(2)}) collective-permute-start(f32[2,64,72]{2,1,0:T(8,128)S(1)} %get-tuple-element.25), channel_id=1, source_target_pairs={{0,240},{16,0},{32,16},{48,32},{64,48},{80,64},{96,80},{112,96},{1... | collective-permute-start | bytes 110600 | tf_op jit(solution)/shard_map/ppermute | solution.py:371
  4.9 4.8 %collective-permute-start = (f32[2,64,72]{2,1,0:T(8,128)S(1)}, f32[2,64,72]{2,1,0:T(8,128)S(1)}, u32[]{:S(2)}, u32[]{:S(2)}) collective-permute-start(f32[2,64,72]{2,1,0:T(8,128)S(1)} %get-tuple-element.26), channel_id=1, source_target_pairs={{0,16},{16,32},{32,48},{48,64},{64,80},{80,96},{96,112},{112,128},... | collective-permute-start | bytes 110600 | tf_op jit(solution)/shard_map/ppermute | solution.py:370
  7.0 24.5 %copy-start.5 = (s32[34]{0:T(128)}, s32[34]{0:T(128)S(1)}, u32[]{:S(2)}) copy-start(s32[34]{0:T(128)S(1)} %pad_add_fusion.1.refs_0_.scalars_ref) | copy-start | bytes 412
  7.0 1.2 %copy-start.2 = (f32[4,4,128,128]{3,2,1,0:T(8,128)S(1)}, f32[4,4,128,128]{3,2,1,0:T(8,128)}, u32[]{:S(2)}) copy-start(f32[4,4,128,128]{3,2,1,0:T(8,128)} %param.6) | copy-start | bytes 3145732
  9.7 33.3 %copy-start.1 = (f32[2,2,128,128]{3,2,1,0:T(8,128)S(1)}, f32[2,2,128,128]{3,2,1,0:T(8,128)}, u32[]{:S(2)}) copy-start(f32[2,2,128,128]{3,2,1,0:T(8,128)} %param.9) | copy-start | bytes 786436
  9.7 33.3 %copy-start.3 = (f32[4,4,128,128]{3,2,1,0:T(8,128)S(1)}, f32[4,4,128,128]{3,2,1,0:T(8,128)}, u32[]{:S(2)}) copy-start(f32[4,4,128,128]{3,2,1,0:T(8,128)} %param.6) | copy-start | bytes 3145732
  9.7 33.3 %copy-start.4 = (bf16[4,128,128]{2,1,0:T(8,128)(2,1)S(1)}, bf16[4,128,128]{2,1,0:T(8,128)(2,1)}, u32[]{:S(2)}) copy-start(bf16[4,128,128]{2,1,0:T(8,128)(2,1)} %constant.18.clone.tables_ref.refs_7_) | copy-start | bytes 393220
  9.7 33.3 %copy-start.7 = (f32[2,128,128]{2,1,0:T(8,128)S(1)}, f32[2,128,128]{2,1,0:T(8,128)}, u32[]{:S(2)}) copy-start(f32[2,128,128]{2,1,0:T(8,128)} %constant.19.clone.refs_6_) | copy-start | bytes 393220
  10.9 19.7 %collective-permute-start.2 = (f32[2,200,64]{2,1,0:T(8,128)S(1)}, f32[2,200,64]{2,1,0:T(8,128)S(1)}, u32[]{:S(2)}, u32[]{:S(2)}) collective-permute-start(f32[2,200,64]{2,1,0:T(8,128)S(1)} %get-tuple-element.20), channel_id=1, source_target_pairs={{0,1},{1,2},{2,3},{3,4},{4,5},{5,6},{6,7},{7,8},{8,9},{9,10},{10,1... | collective-permute-start | bytes 307208 | tf_op jit(solution)/shard_map/ppermute | solution.py:386
  11.9 18.6 %collective-permute-start.3 = (f32[2,200,64]{2,1,0:T(8,128)S(1)}, f32[2,200,64]{2,1,0:T(8,128)S(1)}, u32[]{:S(2)}, u32[]{:S(2)}) collective-permute-start(f32[2,200,64]{2,1,0:T(8,128)S(1)} %get-tuple-element.21), channel_id=1, source_target_pairs={{0,15},{1,0},{2,1},{3,2},{4,3},{5,4},{6,5},{7,6},{8,7},{9,8},{10,9... | collective-permute-start | bytes 307208 | tf_op jit(solution)/shard_map/ppermute | solution.py:387
  17.3 25.7 %all-to-all-start = ((f32[256,1,128]{2,1,0:T(1,128)}), f32[256,1,128]{2,1,0:T(1,128)S(1)}, u32[]{:S(2)}, u32[]{:S(2)}) async-start(f32[256,1,128]{2,1,0:T(1,128)} %bitcast.4), calls=%async_computation | async-start | bytes 262144 | tf_op jit(solution)/shard_map/all_to_all | solution.py:336
  31.5 11.6 %copy-start = (f32[4,200,128]{2,1,0:T(8,128)S(1)}, f32[4,200,128]{2,1,0:T(8,128)}, u32[]{:S(2)}) copy-start(f32[4,200,128]{2,1,0:T(8,128)} %maximum_maximum_fusion.ext_ref.refs_4_) | copy-start | bytes 1228804
  43.1 0.7 copy-start.6
  43.7 47.0 %copy-start.8 = (f32[2,72,72]{2,1,0:T(8,128)S(1)}, f32[2,72,72]{2,1,0:T(8,128)}, u32[]{:S(2)}) copy-start(f32[2,72,72]{2,1,0:T(8,128)} %param.8) | copy-start | bytes 124420
  54.3 14.0 %all-to-all-start.1 = ((f32[32,16,128]{2,1,0:T(8,128)}), f32[32,16,128]{2,1,0:T(8,128)S(1)}, u32[]{:S(2)}, u32[]{:S(2)}) async-start(f32[32,16,128]{2,1,0:T(8,128)} %bitcast.7), calls=%async_computation.1 | async-start | bytes 524288 | tf_op jit(solution)/shard_map/all_to_all | solution.py:336
  59.3 17.2 %collective-permute-start.5 = (f32[4,64,128]{2,1,0:T(8,128)S(1)}, f32[4,64,128]{2,1,0:T(8,128)S(1)}, u32[]{:S(2)}, u32[]{:S(2)}) collective-permute-start(f32[4,64,128]{2,1,0:T(8,128)S(1)} %get-tuple-element.18), channel_id=1, source_target_pairs={{0,16},{16,32},{32,48},{48,64},{64,80},{80,96},{96,112},{112,128},... | collective-permute-start | bytes 393224 | tf_op jit(solution)/shard_map/ppermute | solution.py:435
  62.5 14.0 %collective-permute-start.4 = (f32[4,64,128]{2,1,0:T(8,128)S(1)}, f32[4,64,128]{2,1,0:T(8,128)S(1)}, u32[]{:S(2)}, u32[]{:S(2)}) collective-permute-start(f32[4,64,128]{2,1,0:T(8,128)S(1)} %get-tuple-element.19), channel_id=1, source_target_pairs={{0,240},{16,0},{32,16},{48,32},{64,48},{80,64},{96,80},{112,96},{1... | collective-permute-start | bytes 393224 | tf_op jit(solution)/shard_map/ppermute | solution.py:434
  69.0 14.7 %all-to-all-start.2 = ((f32[8,16,128]{2,1,0:T(8,128)}), f32[8,16,128]{2,1,0:T(8,128)S(1)}, u32[]{:S(2)}, u32[]{:S(2)}) async-start(f32[8,16,128]{2,1,0:T(8,128)} %broadcast_in_dim.7), calls=%async_computation.2 | async-start | bytes 131072 | tf_op jit(solution)/shard_map/all_to_all | solution.py:336
  76.6 14.1 %collective-permute-start.7 = (f32[2,72,64]{2,1,0:T(8,128)S(1)}, f32[2,72,64]{2,1,0:T(8,128)S(1)}, u32[]{:S(2)}, u32[]{:S(2)}) collective-permute-start(f32[2,72,64]{2,1,0:T(8,128)S(1)} %get-tuple-element.22), channel_id=1, source_target_pairs={{0,1},{1,2},{2,3},{3,4},{4,5},{5,6},{6,7},{7,8},{8,9},{9,10},{10,1... | collective-permute-start | bytes 110600 | tf_op jit(solution)/shard_map/ppermute | solution.py:447
  76.7 14.0 %collective-permute-start.6 = (f32[2,72,64]{2,1,0:T(8,128)S(1)}, f32[2,72,64]{2,1,0:T(8,128)S(1)}, u32[]{:S(2)}, u32[]{:S(2)}) collective-permute-start(f32[2,72,64]{2,1,0:T(8,128)S(1)} %get-tuple-element.23), channel_id=1, source_target_pairs={{0,15},{1,0},{2,1},{3,2},{4,3},{5,4},{6,5},{7,6},{8,7},{9,8},{10,9... | collective-permute-start | bytes 110600 | tf_op jit(solution)/shard_map/ppermute | solution.py:446
  84.4 14.9 %all-to-all-start.3 = ((f32[32,16,128]{2,1,0:T(8,128)}), f32[32,16,128]{2,1,0:T(8,128)S(1)}, u32[]{:S(2)}, u32[]{:S(2)}) async-start(f32[32,16,128]{2,1,0:T(8,128)} %broadcast_in_dim.8), calls=%async_computation.3 | async-start | bytes 524288 | tf_op jit(solution)/shard_map/all_to_all | solution.py:336

commit v4 on v3

--- a/solution.py
+++ b/solution.py
@@ -113,7 +113,8 @@
     return (row + 0.5) / (PR * row_dev) - 0.5, (col + 0.5) / (PC * col_dev) - 0.5
 
 
-def sums_kernel(row_dev, col_dev, scalars_ref, patterns_ref, out_ref, total_ref, tilt_ref):
+def sums_kernel(row_dev, col_dev, scalars_ref, patterns_ref, tile_ref, out_ref, tile_out, total_ref, tilt_ref):
+    tile_out[...] = tile_ref[...]
     k = row_iota((W, W))
     freq = (((k + HALF) % W) - HALF).astype(f32)
     for p in range(POSITIONS):
@@ -367,22 +368,27 @@
     tables = jnp.asarray(dft_tables())
     shifts = jnp.asarray(shift_tables())
 
-    above = lax.ppermute(object_field[:, TILE - HALF :, :], "srow", shifted_to("srow", 1))
-    below = lax.ppermute(object_field[:, :HALF, :], "srow", shifted_to("srow", -1))
-
-    sums = pl.pallas_call(
+    above = lax.ppermute(object_field, "srow", shifted_to("srow", 1))
+    below = lax.ppermute(object_field, "srow", shifted_to("srow", -1))
+
+    sums, tile = pl.pallas_call(
         lambda *refs: sums_kernel(row_dev, col_dev, *refs),
-        out_shape=jax.ShapeDtypeStruct((row_dev * col_dev, W), f32),
-        in_specs=[SMEM, VMEM],
-        out_specs=VMEM,
+        out_shape=(
+            jax.ShapeDtypeStruct((row_dev * col_dev, W), f32),
+            jax.ShapeDtypeStruct(object_field.shape, f32),
+        ),
+        in_specs=[SMEM, VMEM, VMEM],
+        out_specs=(VMEM, VMEM),
         scratch_shapes=[pltpu.VMEM((POSITIONS, W), f32), pltpu.VMEM((POSITIONS, W), f32)],
         compiler_params=params(8),
         name="sums",
-    )(scalars, patterns)
+    )(scalars, patterns, object_field)
     above, below, _ = lax.optimization_barrier((above, below, sums))
     sums = spread(sums.reshape(row_dev * col_dev, 1, W)).reshape(row_dev * col_dev, W)
 
-    tall = jnp.concatenate([above, object_field, below], axis=1)
+    tall = jnp.concatenate(
+        [above[:, TILE - HALF :, :], tile, below[:, :HALF, :]], axis=1
+    )
     left_rim = lax.ppermute(tall[:, :, TILE - HALF :], "scol", shifted_to("scol", 1))
     right_rim = lax.ppermute(tall[:, :, :HALF], "scol", shifted_to("scol", -1))
 
@@ -406,6 +412,9 @@
         cost_estimate=pl.CostEstimate(flops=0, bytes_accessed=0, transcendentals=0),
         name="forward",
     )(scalars, ext, probe_flat, tables)
+
+    again, sums = lax.optimization_barrier((offsets, sums))
+    scalars = jnp.concatenate([again.reshape(2 * POSITIONS), place])
 
     ext_grad, probe_grad = pl.pallas_call(
         lambda *refs: backward_kernel(row_dev, col_dev, *refs),

time: 101 us -> 98.5 us (0.975)
  starting transfers between devices: 49.4 us -> 46.9 us
  waiting for transfers between devices: 19.7 us -> 21.4 us
  local copies, waits for them, and re-layouts: 6.51 us -> 5.02 us
    ppermute x2, waiting for transfers between devices: 0.01 us -> 1.75 us  [the longest x1 1.74 us: on_device(): below = lax.ppermute(object_field, 'srow', shifted_to('srow', -1))]
    all_to_all x4, starting transfers between devices: 31.6 us -> 30.3 us  [spread(): lax.all_to_all(values, ('srow', 'scol'), 0, 0, axis_index_groups=groups,...]
  transfers between devices with their start and end apart: 12 -> 12, of which waited for: 4 -> 5; matrix products, arithmetic and copies ran while one was open for 4% -> 4% of each run, Pallas kernels for 10% -> 11%
where the time goes in v4:
time: 98.5 us; the launch traced here: 98 us
  starting transfers between devices  46.9 us (48%)
  waiting for transfers between devices  21.4 us (22%)
  Pallas kernels  21 us (21%)
  local copies, waits for them, and re-layouts  5.02 us (5%)
  other arithmetic  2.69 us (3%)
    all_to_all x4, starting transfers between devices, spread(): lax.all_to_all(values, ('srow', 'scol'), 0, 0, axis_index_groups=groups,...  30.3 us
    all_to_all x4, waiting for transfers between devices, spread(): lax.all_to_all(values, ('srow', 'scol'), 0, 0, axis_index_groups=groups,...  19.7 us
    pallas_call x1, Pallas kernels, on_device(): pl.pallas_call(lambda *refs: backward_kernel(row_dev, col_dev, *refs), ou...  10.6 us
    pallas_call x1, Pallas kernels, on_device(): pl.pallas_call(forward_kernel, out_shape=jax.ShapeDtypeStruct((POSITIONS,...  8.97 us
    ppermute x1, starting transfers between devices, on_device(): right_rim = lax.ppermute(tall[:, :, :HALF], 'scol', shifted_to('scol', -1))  5.28 us
    ppermute x1, starting transfers between devices, on_device(): above = lax.ppermute(object_field, 'srow', shifted_to('srow', 1))  4.38 us
    ppermute x1, starting transfers between devices, on_device(): lax.ppermute(grad[:2, :, :HALF], 'scol', shifted_to('scol', -1))  3.56 us
    ppermute x1, starting transfers between devices, on_device(): lax.ppermute(ext_grad[:, HALF + TILE:, :], 'srow', shifted_to('srow', 1))  3.21 us
  transfers between devices with their start and end apart: 12, of which 5 were waited for; matrix products, arithmetic and copies ran while one was open for 4% of the time, Pallas kernels for 11%

profile of v4, /device:TPU:1, one launch (start us, length us, event | category | flops | bytes accessed | tf_op | source)
XLA Modules:
  0.0 98.0 jit_solution(11649155846711997446)
XLA Ops:
  0.6 4.4 %collective-permute-start = (f32[2,72,72]{2,1,0:T(8,128)}, f32[2,72,72]{2,1,0:T(8,128)S(1)}, u32[]{:S(2)}, u32[]{:S(2)}) collective-permute-start(f32[2,72,72]{2,1,0:T(8,128)} %refs_2_.1), channel_id=1, source_target_pairs={{0,16},{16,32},{32,48},{48,64},{64,80},{80,96},{96,112},{112,128},... | collective-permute-start | bytes 124424 | tf_op jit(solution)/shard_map/ppermute | solution.py:371
  5.0 0.8 copy.15
  6.0 1.2 %copy-done.2 = f32[4,4,128,128]{3,2,1,0:T(8,128)S(1)} copy-done((f32[4,4,128,128]{3,2,1,0:T(8,128)S(1)}, f32[4,4,128,128]{3,2,1,0:T(8,128)}, u32[]{:S(2)}) %copy-start.2) | copy-done | bytes 1048600
  7.2 0.9 copy-done.4
  8.1 1.4 %sums.1 = (f32[256,128]{1,0:T(8,128)}, f32[2,72,72]{2,1,0:T(8,128)S(1)}) custom-call(s32[34]{0:T(128)S(1)} %add_add_fusion.refs_0_.scalars_ref, f32[16,128,128]{2,1,0:T(8,128)S(1)} %bitcast.12, f32[2,72,72]{2,1,0:T(8,128)S(1)} %copy-done.4), custom_call_target="tpu_custom_call" | custom-call | tf_op jit(solution)/shard_map/sums/pallas_call | solution.py:374
  9.5 1.7 %collective-permute-done.1 = f32[2,72,72]{2,1,0:T(8,128)S(1)} collective-permute-done((f32[2,72,72]{2,1,0:T(8,128)}, f32[2,72,72]{2,1,0:T(8,128)S(1)}, u32[]{:S(2)}, u32[]{:S(2)}) %collective-permute-start.1) | collective-permute-done | bytes 41504 | tf_op jit(solution)/shard_map/ppermute | solution.py:372
  11.6 5.3 %collective-permute-start.3 = (f32[2,200,64]{2,1,0:T(8,128)S(1)}, f32[2,200,64]{2,1,0:T(8,128)S(1)}, u32[]{:S(2)}, u32[]{:S(2)}) collective-permute-start(f32[2,200,64]{2,1,0:T(8,128)S(1)} %get-tuple-element.29), channel_id=1, source_target_pairs={{0,15},{1,0},{2,1},{3,2},{4,3},{5,4},{6,5},{7,6},{8,7},{9,8},{10,9... | collective-permute-start | bytes 307208 | tf_op jit(solution)/shard_map/ppermute | solution.py:393
  16.9 11.7 %all-to-all-start = ((f32[256,1,128]{2,1,0:T(1,128)}), f32[256,1,128]{2,1,0:T(1,128)S(1)}, u32[]{:S(2)}, u32[]{:S(2)}) async-start(f32[256,1,128]{2,1,0:T(1,128)} %bitcast.4), calls=%async_computation | async-start | bytes 262144 | tf_op jit(solution)/shard_map/all_to_all | solution.py:337
  28.8 0.9 maximum_maximum_fusion.ext_ref.refs_4_
  29.8 9.0 %forward.1.refs_3_ = f32[16,256,256]{2,1,0:T(8,128)} custom-call(s32[34]{0:T(128)} %copy-done.7, f32[4,200,128]{2,1,0:T(8,128)} %maximum_maximum_fusion.ext_ref.refs_4_, f32[4,128,128]{2,1,0:T(8,128)} %bitcast.10, bf16[4,128,128]{2,1,0:T(8,128)(2,1)} %constant.18.clone.tables_ref.refs_7_), custom_call_target="tpu_custom_call" | custom-call | tf_op jit(solution)/shard_map/forward/pallas_call | solution.py:401
  38.7 2.6 %all-to-all-done = f32[256,1,128]{2,1,0:T(1,128)S(1)} async-done(((f32[256,1,128]{2,1,0:T(1,128)}), f32[256,1,128]{2,1,0:T(1,128)S(1)}, u32[]{:S(2)}, u32[]{:S(2)}) %all-to-all-start) | async-done | bytes 131104 | tf_op jit(solution)/shard_map/all_to_all | solution.py:337
  41.6 10.6 %backward.1 = (f32[4,200,128]{2,1,0:T(8,128)S(1)}, f32[4,128,128]{2,1,0:T(8,128)}) custom-call(s32[34]{0:T(128)S(1)} %add_add_fusion.1.refs_0_, f32[256,128]{1,0:T(8,128)S(1)} %bitcast.14, f32[16,128,128]{2,1,0:T(8,128)S(1)} %bitcast.13, f32[16,256,256]{2,1,0:T(8,128)} %forward.1.refs_3_, f32[4,200,128]{2,1,0:T(8,128)S(1)} %copy-done, ...), custom_call_target="tpu_custom_call" | custom-call | flops 8589934592 | bytes 9437184 | tf_op jit(solution)/shard_map/backward/pallas_call | solution.py:419
  52.3 4.9 %all-to-all-start.1 = ((f32[32,16,128]{2,1,0:T(8,128)}), f32[32,16,128]{2,1,0:T(8,128)S(1)}, u32[]{:S(2)}, u32[]{:S(2)}) async-start(f32[32,16,128]{2,1,0:T(8,128)} %bitcast.7), calls=%async_computation.1 | async-start | bytes 524288 | tf_op jit(solution)/shard_map/all_to_all | solution.py:337
  57.2 3.2 %collective-permute-start.5 = (f32[4,64,128]{2,1,0:T(8,128)S(1)}, f32[4,64,128]{2,1,0:T(8,128)S(1)}, u32[]{:S(2)}, u32[]{:S(2)}) collective-permute-start(f32[4,64,128]{2,1,0:T(8,128)S(1)} %get-tuple-element.26), channel_id=1, source_target_pairs={{0,16},{16,32},{32,48},{48,64},{64,80},{80,96},{96,112},{112,128},... | collective-permute-start | bytes 393224 | tf_op jit(solution)/shard_map/ppermute | solution.py:444
  60.4 5.9 %all-to-all-done.1 = f32[32,16,128]{2,1,0:T(8,128)S(1)} async-done(((f32[32,16,128]{2,1,0:T(8,128)}), f32[32,16,128]{2,1,0:T(8,128)S(1)}, u32[]{:S(2)}, u32[]{:S(2)}) %all-to-all-start.1) | async-done | bytes 262176 | tf_op jit(solution)/shard_map/all_to_all | solution.py:337
  66.3 0.6 broadcast_in_dim.7
  66.9 7.4 %all-to-all-start.2 = ((f32[8,16,128]{2,1,0:T(8,128)}), f32[8,16,128]{2,1,0:T(8,128)S(1)}, u32[]{:S(2)}, u32[]{:S(2)}) async-start(f32[8,16,128]{2,1,0:T(8,128)} %broadcast_in_dim.7), calls=%async_computation.2 | async-start | bytes 131072 | tf_op jit(solution)/shard_map/all_to_all | solution.py:337
  74.6 3.6 %collective-permute-start.6 = (f32[2,72,64]{2,1,0:T(8,128)S(1)}, f32[2,72,64]{2,1,0:T(8,128)S(1)}, u32[]{:S(2)}, u32[]{:S(2)}) collective-permute-start(f32[2,72,64]{2,1,0:T(8,128)S(1)} %get-tuple-element.31), channel_id=1, source_target_pairs={{0,15},{1,0},{2,1},{3,2},{4,3},{5,4},{6,5},{7,6},{8,7},{9,8},{10,9... | collective-permute-start | bytes 110600 | tf_op jit(solution)/shard_map/ppermute | solution.py:455
  78.2 3.4 %all-to-all-done.2 = f32[8,16,128]{2,1,0:T(8,128)S(1)} async-done(((f32[8,16,128]{2,1,0:T(8,128)}), f32[8,16,128]{2,1,0:T(8,128)S(1)}, u32[]{:S(2)}, u32[]{:S(2)}) %all-to-all-start.2) | async-done | bytes 65568 | tf_op jit(solution)/shard_map/all_to_all | solution.py:337
  81.6 0.7 broadcast_in_dim.8
  82.4 6.3 %all-to-all-start.3 = ((f32[32,16,128]{2,1,0:T(8,128)}), f32[32,16,128]{2,1,0:T(8,128)S(1)}, u32[]{:S(2)}, u32[]{:S(2)}) async-start(f32[32,16,128]{2,1,0:T(8,128)} %broadcast_in_dim.8), calls=%async_computation.3 | async-start | bytes 524288 | tf_op jit(solution)/shard_map/all_to_all | solution.py:337
  88.7 0.7 fusion.1
  89.4 7.8 %all-to-all-done.3 = f32[32,16,128]{2,1,0:T(8,128)S(1)} async-done(((f32[32,16,128]{2,1,0:T(8,128)}), f32[32,16,128]{2,1,0:T(8,128)S(1)}, u32[]{:S(2)}, u32[]{:S(2)}) %all-to-all-start.3) | async-done | bytes 262176 | tf_op jit(solution)/shard_map/all_to_all | solution.py:337
  97.3 0.7 sub.7
  (48 shorter events, 1.2 us)
Async XLA Ops:
  0.6 8.9 %collective-permute-start = (f32[2,72,72]{2,1,0:T(8,128)}, f32[2,72,72]{2,1,0:T(8,128)S(1)}, u32[]{:S(2)}, u32[]{:S(2)}) collective-permute-start(f32[2,72,72]{2,1,0:T(8,128)} %refs_2_.1), channel_id=1, source_target_pairs={{0,16},{16,32},{32,48},{48,64},{64,80},{80,96},{96,112},{112,128},... | collective-permute-start | bytes 124424 | tf_op jit(solution)/shard_map/ppermute | solution.py:371
  5.0 6.3 %collective-permute-start.1 = (f32[2,72,72]{2,1,0:T(8,128)}, f32[2,72,72]{2,1,0:T(8,128)S(1)}, u32[]{:S(2)}, u32[]{:S(2)}) collective-permute-start(f32[2,72,72]{2,1,0:T(8,128)} %refs_2_.1), channel_id=1, source_target_pairs={{0,240},{16,0},{32,16},{48,32},{64,48},{80,64},{96,80},{112,96},{1... | collective-permute-start | bytes 124424 | tf_op jit(solution)/shard_map/ppermute | solution.py:372
  6.0 23.8 %copy-start.7 = (s32[34]{0:T(128)}, s32[34]{0:T(128)S(1)}, u32[]{:S(2)}) copy-start(s32[34]{0:T(128)S(1)} %add_add_fusion.refs_0_.scalars_ref) | copy-start | bytes 412
  6.0 1.2 %copy-start.2 = (f32[4,4,128,128]{3,2,1,0:T(8,128)S(1)}, f32[4,4,128,128]{3,2,1,0:T(8,128)}, u32[]{:S(2)}) copy-start(f32[4,4,128,128]{3,2,1,0:T(8,128)} %param.6) | copy-start | bytes 3145732
  7.2 0.9 copy-start.4
  11.3 30.0 %copy-start.9 = (s32[4,4,2]{1,2,0:T(2,128)S(1)}, s32[4,4,2]{1,2,0:T(2,128)}, u32[]{:S(2)}) copy-start(s32[4,4,2]{1,2,0:T(2,128)} %param.7) | copy-start | bytes 388
  11.3 30.3 %copy-start.1 = (f32[2,2,128,128]{3,2,1,0:T(8,128)S(1)}, f32[2,2,128,128]{3,2,1,0:T(8,128)}, u32[]{:S(2)}) copy-start(f32[2,2,128,128]{3,2,1,0:T(8,128)} %param.9) | copy-start | bytes 786436
  11.3 30.3 %copy-start.3 = (f32[4,4,128,128]{3,2,1,0:T(8,128)S(1)}, f32[4,4,128,128]{3,2,1,0:T(8,128)}, u32[]{:S(2)}) copy-start(f32[4,4,128,128]{3,2,1,0:T(8,128)} %param.6) | copy-start | bytes 3145732
  11.3 30.3 %copy-start.6 = (bf16[4,128,128]{2,1,0:T(8,128)(2,1)S(1)}, bf16[4,128,128]{2,1,0:T(8,128)(2,1)}, u32[]{:S(2)}) copy-start(bf16[4,128,128]{2,1,0:T(8,128)(2,1)} %constant.18.clone.tables_ref.refs_7_) | copy-start | bytes 393220
  11.3 30.3 %copy-start.8 = (f32[2,128,128]{2,1,0:T(8,128)S(1)}, f32[2,128,128]{2,1,0:T(8,128)}, u32[]{:S(2)}) copy-start(f32[2,128,128]{2,1,0:T(8,128)} %constant.19.clone.refs_6_) | copy-start | bytes 393220
  11.5 17.3 %collective-permute-start.2 = (f32[2,200,64]{2,1,0:T(8,128)S(1)}, f32[2,200,64]{2,1,0:T(8,128)S(1)}, u32[]{:S(2)}, u32[]{:S(2)}) collective-permute-start(f32[2,200,64]{2,1,0:T(8,128)S(1)} %get-tuple-element.28), channel_id=1, source_target_pairs={{0,1},{1,2},{2,3},{3,4},{4,5},{5,6},{6,7},{7,8},{8,9},{9,10},{10,1... | collective-permute-start | bytes 307208 | tf_op jit(solution)/shard_map/ppermute | solution.py:392
  11.6 17.2 %collective-permute-start.3 = (f32[2,200,64]{2,1,0:T(8,128)S(1)}, f32[2,200,64]{2,1,0:T(8,128)S(1)}, u32[]{:S(2)}, u32[]{:S(2)}) collective-permute-start(f32[2,200,64]{2,1,0:T(8,128)S(1)} %get-tuple-element.29), channel_id=1, source_target_pairs={{0,15},{1,0},{2,1},{3,2},{4,3},{5,4},{6,5},{7,6},{8,7},{9,8},{10,9... | collective-permute-start | bytes 307208 | tf_op jit(solution)/shard_map/ppermute | solution.py:393
  16.9 24.4 %all-to-all-start = ((f32[256,1,128]{2,1,0:T(1,128)}), f32[256,1,128]{2,1,0:T(1,128)S(1)}, u32[]{:S(2)}, u32[]{:S(2)}) async-start(f32[256,1,128]{2,1,0:T(1,128)} %bitcast.4), calls=%async_computation | async-start | bytes 262144 | tf_op jit(solution)/shard_map/all_to_all | solution.py:337
  29.8 11.9 %copy-start = (f32[4,200,128]{2,1,0:T(8,128)S(1)}, f32[4,200,128]{2,1,0:T(8,128)}, u32[]{:S(2)}) copy-start(f32[4,200,128]{2,1,0:T(8,128)} %maximum_maximum_fusion.ext_ref.refs_4_) | copy-start | bytes 1228804
  41.6 47.0 %copy-start.5 = (f32[2,72,72]{2,1,0:T(8,128)S(1)}, f32[2,72,72]{2,1,0:T(8,128)}, u32[]{:S(2)}) copy-start(f32[2,72,72]{2,1,0:T(8,128)} %refs_2_.1) | copy-start | bytes 124420
  52.3 14.0 %all-to-all-start.1 = ((f32[32,16,128]{2,1,0:T(8,128)}), f32[32,16,128]{2,1,0:T(8,128)S(1)}, u32[]{:S(2)}, u32[]{:S(2)}) async-start(f32[32,16,128]{2,1,0:T(8,128)} %bitcast.7), calls=%async_computation.1 | async-start | bytes 524288 | tf_op jit(solution)/shard_map/all_to_all | solution.py:337
  57.2 17.2 %collective-permute-start.5 = (f32[4,64,128]{2,1,0:T(8,128)S(1)}, f32[4,64,128]{2,1,0:T(8,128)S(1)}, u32[]{:S(2)}, u32[]{:S(2)}) collective-permute-start(f32[4,64,128]{2,1,0:T(8,128)S(1)} %get-tuple-element.26), channel_id=1, source_target_pairs={{0,16},{16,32},{32,48},{48,64},{64,80},{80,96},{96,112},{112,128},... | collective-permute-start | bytes 393224 | tf_op jit(solution)/shard_map/ppermute | solution.py:444
  60.4 14.0 %collective-permute-start.4 = (f32[4,64,128]{2,1,0:T(8,128)S(1)}, f32[4,64,128]{2,1,0:T(8,128)S(1)}, u32[]{:S(2)}, u32[]{:S(2)}) collective-permute-start(f32[4,64,128]{2,1,0:T(8,128)S(1)} %get-tuple-element.27), channel_id=1, source_target_pairs={{0,240},{16,0},{32,16},{48,32},{64,48},{80,64},{96,80},{112,96},{1... | collective-permute-start | bytes 393224 | tf_op jit(solution)/shard_map/ppermute | solution.py:443
  66.9 14.7 %all-to-all-start.2 = ((f32[8,16,128]{2,1,0:T(8,128)}), f32[8,16,128]{2,1,0:T(8,128)S(1)}, u32[]{:S(2)}, u32[]{:S(2)}) async-start(f32[8,16,128]{2,1,0:T(8,128)} %broadcast_in_dim.7), calls=%async_computation.2 | async-start | bytes 131072 | tf_op jit(solution)/shard_map/all_to_all | solution.py:337
  74.5 14.1 %collective-permute-start.7 = (f32[2,72,64]{2,1,0:T(8,128)S(1)}, f32[2,72,64]{2,1,0:T(8,128)S(1)}, u32[]{:S(2)}, u32[]{:S(2)}) collective-permute-start(f32[2,72,64]{2,1,0:T(8,128)S(1)} %get-tuple-element.30), channel_id=1, source_target_pairs={{0,1},{1,2},{2,3},{3,4},{4,5},{5,6},{6,7},{7,8},{8,9},{9,10},{10,1... | collective-permute-start | bytes 110600 | tf_op jit(solution)/shard_map/ppermute | solution.py:456
  74.6 14.0 %collective-permute-start.6 = (f32[2,72,64]{2,1,0:T(8,128)S(1)}, f32[2,72,64]{2,1,0:T(8,128)S(1)}, u32[]{:S(2)}, u32[]{:S(2)}) collective-permute-start(f32[2,72,64]{2,1,0:T(8,128)S(1)} %get-tuple-element.31), channel_id=1, source_target_pairs={{0,15},{1,0},{2,1},{3,2},{4,3},{5,4},{6,5},{7,6},{8,7},{9,8},{10,9... | collective-permute-start | bytes 110600 | tf_op jit(solution)/shard_map/ppermute | solution.py:455
  82.4 14.9 %all-to-all-start.3 = ((f32[32,16,128]{2,1,0:T(8,128)}), f32[32,16,128]{2,1,0:T(8,128)S(1)}, u32[]{:S(2)}, u32[]{:S(2)}) async-start(f32[32,16,128]{2,1,0:T(8,128)} %broadcast_in_dim.8), calls=%async_computation.3 | async-start | bytes 524288 | tf_op jit(solution)/shard_map/all_to_all | solution.py:337

commit v5 on v4

--- a/solution.py
+++ b/solution.py
@@ -17,7 +17,7 @@
 POSITIONS = PR * PC
 TILE = 72
 EXT = TILE + W
-GROUP = 8
+GROUP = 16
 AHEAD = 8
 
 obj_rate = 0.2

time: 98.5 us -> 98.1 us (level)
  no operation moved by 1% of the time
where the time goes in v5:
time: 98.1 us; the launch traced here: 97.6 us
  starting transfers between devices  47.2 us (48%)
  waiting for transfers between devices  21.1 us (22%)
  Pallas kernels  20.8 us (21%)
  local copies, waits for them, and re-layouts  5.02 us (5%)
  other arithmetic  2.69 us (3%)
    all_to_all x4, starting transfers between devices, spread(): lax.all_to_all(values, ('srow', 'scol'), 0, 0, axis_index_groups=groups,...  30.3 us
    all_to_all x4, waiting for transfers between devices, spread(): lax.all_to_all(values, ('srow', 'scol'), 0, 0, axis_index_groups=groups,...  19.3 us
    pallas_call x1, Pallas kernels, on_device(): pl.pallas_call(lambda *refs: backward_kernel(row_dev, col_dev, *refs), ou...  10.2 us
    pallas_call x1, Pallas kernels, on_device(): pl.pallas_call(forward_kernel, out_shape=jax.ShapeDtypeStruct((POSITIONS,...  9.13 us
    ppermute x1, starting transfers between devices, on_device(): right_rim = lax.ppermute(tall[:, :, :HALF], 'scol', shifted_to('scol', -1))  5.28 us
    ppermute x1, starting transfers between devices, on_device(): above = lax.ppermute(object_field, 'srow', shifted_to('srow', 1))  4.38 us
    ppermute x1, starting transfers between devices, on_device(): lax.ppermute(grad[:2, :, :HALF], 'scol', shifted_to('scol', -1))  3.56 us
    ppermute x1, starting transfers between devices, on_device(): lax.ppermute(ext_grad[:, HALF + TILE:, :], 'srow', shifted_to('srow', 1))  3.43 us
  transfers between devices with their start and end apart: 12, of which 5 were waited for; matrix products, arithmetic and copies ran while one was open for 4% of the time, Pallas kernels for 11%

profile of v5, /device:TPU:1, one launch (start us, length us, event | category | flops | bytes accessed | tf_op | source)
XLA Modules:
  0.0 97.6 jit_solution(8520480924190592891)
XLA Ops:
  0.6 4.4 %collective-permute-start = (f32[2,72,72]{2,1,0:T(8,128)}, f32[2,72,72]{2,1,0:T(8,128)S(1)}, u32[]{:S(2)}, u32[]{:S(2)}) collective-permute-start(f32[2,72,72]{2,1,0:T(8,128)} %refs_2_.1), channel_id=1, source_target_pairs={{0,16},{16,32},{32,48},{48,64},{64,80},{80,96},{96,112},{112,128},... | collective-permute-start | bytes 124424 | tf_op jit(solution)/shard_map/ppermute | solution.py:371
  5.0 0.8 copy.15
  6.0 1.2 %copy-done.2 = f32[4,4,128,128]{3,2,1,0:T(8,128)S(1)} copy-done((f32[4,4,128,128]{3,2,1,0:T(8,128)S(1)}, f32[4,4,128,128]{3,2,1,0:T(8,128)}, u32[]{:S(2)}) %copy-start.2) | copy-done | bytes 1048600
  7.2 0.9 copy-done.4
  8.1 1.4 %sums.1 = (f32[256,128]{1,0:T(8,128)}, f32[2,72,72]{2,1,0:T(8,128)S(1)}) custom-call(s32[34]{0:T(128)S(1)} %add_add_fusion.refs_0_.scalars_ref, f32[16,128,128]{2,1,0:T(8,128)S(1)} %bitcast.12, f32[2,72,72]{2,1,0:T(8,128)S(1)} %copy-done.4), custom_call_target="tpu_custom_call" | custom-call | tf_op jit(solution)/shard_map/sums/pallas_call | solution.py:374
  9.5 1.7 %collective-permute-done.1 = f32[2,72,72]{2,1,0:T(8,128)S(1)} collective-permute-done((f32[2,72,72]{2,1,0:T(8,128)}, f32[2,72,72]{2,1,0:T(8,128)S(1)}, u32[]{:S(2)}, u32[]{:S(2)}) %collective-permute-start.1) | collective-permute-done | bytes 41504 | tf_op jit(solution)/shard_map/ppermute | solution.py:372
  11.6 5.3 %collective-permute-start.3 = (f32[2,200,64]{2,1,0:T(8,128)S(1)}, f32[2,200,64]{2,1,0:T(8,128)S(1)}, u32[]{:S(2)}, u32[]{:S(2)}) collective-permute-start(f32[2,200,64]{2,1,0:T(8,128)S(1)} %get-tuple-element.29), channel_id=1, source_target_pairs={{0,15},{1,0},{2,1},{3,2},{4,3},{5,4},{6,5},{7,6},{8,7},{9,8},{10,9... | collective-permute-start | bytes 307208 | tf_op jit(solution)/shard_map/ppermute | solution.py:393
  16.9 11.7 %all-to-all-start = ((f32[256,1,128]{2,1,0:T(1,128)}), f32[256,1,128]{2,1,0:T(1,128)S(1)}, u32[]{:S(2)}, u32[]{:S(2)}) async-start(f32[256,1,128]{2,1,0:T(1,128)} %bitcast.4), calls=%async_computation | async-start | bytes 262144 | tf_op jit(solution)/shard_map/all_to_all | solution.py:337
  28.8 0.9 maximum_maximum_fusion.ext_ref.refs_4_
  29.8 9.1 %forward.1.refs_3_ = f32[16,256,256]{2,1,0:T(8,128)} custom-call(s32[34]{0:T(128)} %copy-done.7, f32[4,200,128]{2,1,0:T(8,128)} %maximum_maximum_fusion.ext_ref.refs_4_, f32[4,128,128]{2,1,0:T(8,128)} %bitcast.10, bf16[4,128,128]{2,1,0:T(8,128)(2,1)} %constant.18.clone.tables_ref.refs_7_), custom_call_target="tpu_custom_call" | custom-call | tf_op jit(solution)/shard_map/forward/pallas_call | solution.py:401
  38.9 2.4 %all-to-all-done = f32[256,1,128]{2,1,0:T(1,128)S(1)} async-done(((f32[256,1,128]{2,1,0:T(1,128)}), f32[256,1,128]{2,1,0:T(1,128)S(1)}, u32[]{:S(2)}, u32[]{:S(2)}) %all-to-all-start) | async-done | bytes 131104 | tf_op jit(solution)/shard_map/all_to_all | solution.py:337
  41.6 10.2 %backward.1 = (f32[4,200,128]{2,1,0:T(8,128)S(1)}, f32[4,128,128]{2,1,0:T(8,128)}) custom-call(s32[34]{0:T(128)S(1)} %add_add_fusion.1.refs_0_, f32[256,128]{1,0:T(8,128)S(1)} %bitcast.14, f32[16,128,128]{2,1,0:T(8,128)S(1)} %bitcast.13, f32[16,256,256]{2,1,0:T(8,128)} %forward.1.refs_3_, f32[4,200,128]{2,1,0:T(8,128)S(1)} %copy-done, ...), custom_call_target="tpu_custom_call" | custom-call | flops 8589934592 | bytes 9437184 | tf_op jit(solution)/shard_map/backward/pallas_call | solution.py:419
  51.9 4.9 %all-to-all-start.1 = ((f32[32,16,128]{2,1,0:T(8,128)}), f32[32,16,128]{2,1,0:T(8,128)S(1)}, u32[]{:S(2)}, u32[]{:S(2)}) async-start(f32[32,16,128]{2,1,0:T(8,128)} %bitcast.7), calls=%async_computation.1 | async-start | bytes 524288 | tf_op jit(solution)/shard_map/all_to_all | solution.py:337
  56.8 3.4 %collective-permute-start.5 = (f32[4,64,128]{2,1,0:T(8,128)S(1)}, f32[4,64,128]{2,1,0:T(8,128)S(1)}, u32[]{:S(2)}, u32[]{:S(2)}) collective-permute-start(f32[4,64,128]{2,1,0:T(8,128)S(1)} %get-tuple-element.26), channel_id=1, source_target_pairs={{0,16},{16,32},{32,48},{48,64},{64,80},{80,96},{96,112},{112,128},... | collective-permute-start | bytes 393224 | tf_op jit(solution)/shard_map/ppermute | solution.py:444
  60.3 5.7 %all-to-all-done.1 = f32[32,16,128]{2,1,0:T(8,128)S(1)} async-done(((f32[32,16,128]{2,1,0:T(8,128)}), f32[32,16,128]{2,1,0:T(8,128)S(1)}, u32[]{:S(2)}, u32[]{:S(2)}) %all-to-all-start.1) | async-done | bytes 262176 | tf_op jit(solution)/shard_map/all_to_all | solution.py:337
  66.0 0.6 broadcast_in_dim.7
  66.6 7.4 %all-to-all-start.2 = ((f32[8,16,128]{2,1,0:T(8,128)}), f32[8,16,128]{2,1,0:T(8,128)S(1)}, u32[]{:S(2)}, u32[]{:S(2)}) async-start(f32[8,16,128]{2,1,0:T(8,128)} %broadcast_in_dim.7), calls=%async_computation.2 | async-start | bytes 131072 | tf_op jit(solution)/shard_map/all_to_all | solution.py:337
  74.3 3.6 %collective-permute-start.6 = (f32[2,72,64]{2,1,0:T(8,128)S(1)}, f32[2,72,64]{2,1,0:T(8,128)S(1)}, u32[]{:S(2)}, u32[]{:S(2)}) collective-permute-start(f32[2,72,64]{2,1,0:T(8,128)S(1)} %get-tuple-element.31), channel_id=1, source_target_pairs={{0,15},{1,0},{2,1},{3,2},{4,3},{5,4},{6,5},{7,6},{8,7},{9,8},{10,9... | collective-permute-start | bytes 110600 | tf_op jit(solution)/shard_map/ppermute | solution.py:455
  77.8 3.4 %all-to-all-done.2 = f32[8,16,128]{2,1,0:T(8,128)S(1)} async-done(((f32[8,16,128]{2,1,0:T(8,128)}), f32[8,16,128]{2,1,0:T(8,128)S(1)}, u32[]{:S(2)}, u32[]{:S(2)}) %all-to-all-start.2) | async-done | bytes 65568 | tf_op jit(solution)/shard_map/all_to_all | solution.py:337
  81.3 0.7 broadcast_in_dim.8
  82.0 6.3 %all-to-all-start.3 = ((f32[32,16,128]{2,1,0:T(8,128)}), f32[32,16,128]{2,1,0:T(8,128)S(1)}, u32[]{:S(2)}, u32[]{:S(2)}) async-start(f32[32,16,128]{2,1,0:T(8,128)} %broadcast_in_dim.8), calls=%async_computation.3 | async-start | bytes 524288 | tf_op jit(solution)/shard_map/all_to_all | solution.py:337
  88.3 0.7 fusion.1
  89.0 7.8 %all-to-all-done.3 = f32[32,16,128]{2,1,0:T(8,128)S(1)} async-done(((f32[32,16,128]{2,1,0:T(8,128)}), f32[32,16,128]{2,1,0:T(8,128)S(1)}, u32[]{:S(2)}, u32[]{:S(2)}) %all-to-all-start.3) | async-done | bytes 262176 | tf_op jit(solution)/shard_map/all_to_all | solution.py:337
  96.9 0.7 sub.7
  (48 shorter events, 1.2 us)
Async XLA Ops:
  0.6 8.9 %collective-permute-start = (f32[2,72,72]{2,1,0:T(8,128)}, f32[2,72,72]{2,1,0:T(8,128)S(1)}, u32[]{:S(2)}, u32[]{:S(2)}) collective-permute-start(f32[2,72,72]{2,1,0:T(8,128)} %refs_2_.1), channel_id=1, source_target_pairs={{0,16},{16,32},{32,48},{48,64},{64,80},{80,96},{96,112},{112,128},... | collective-permute-start | bytes 124424 | tf_op jit(solution)/shard_map/ppermute | solution.py:371
  5.0 6.3 %collective-permute-start.1 = (f32[2,72,72]{2,1,0:T(8,128)}, f32[2,72,72]{2,1,0:T(8,128)S(1)}, u32[]{:S(2)}, u32[]{:S(2)}) collective-permute-start(f32[2,72,72]{2,1,0:T(8,128)} %refs_2_.1), channel_id=1, source_target_pairs={{0,240},{16,0},{32,16},{48,32},{64,48},{80,64},{96,80},{112,96},{1... | collective-permute-start | bytes 124424 | tf_op jit(solution)/shard_map/ppermute | solution.py:372
  6.0 23.8 %copy-start.7 = (s32[34]{0:T(128)}, s32[34]{0:T(128)S(1)}, u32[]{:S(2)}) copy-start(s32[34]{0:T(128)S(1)} %add_add_fusion.refs_0_.scalars_ref) | copy-start | bytes 412
  6.0 1.2 %copy-start.2 = (f32[4,4,128,128]{3,2,1,0:T(8,128)S(1)}, f32[4,4,128,128]{3,2,1,0:T(8,128)}, u32[]{:S(2)}) copy-start(f32[4,4,128,128]{3,2,1,0:T(8,128)} %param.6) | copy-start | bytes 3145732
  7.2 0.9 copy-start.4
  11.3 30.0 %copy-start.9 = (s32[4,4,2]{1,2,0:T(2,128)S(1)}, s32[4,4,2]{1,2,0:T(2,128)}, u32[]{:S(2)}) copy-start(s32[4,4,2]{1,2,0:T(2,128)} %param.7) | copy-start | bytes 388
  11.3 30.3 %copy-start.1 = (f32[2,2,128,128]{3,2,1,0:T(8,128)S(1)}, f32[2,2,128,128]{3,2,1,0:T(8,128)}, u32[]{:S(2)}) copy-start(f32[2,2,128,128]{3,2,1,0:T(8,128)} %param.9) | copy-start | bytes 786436
  11.3 30.3 %copy-start.3 = (f32[4,4,128,128]{3,2,1,0:T(8,128)S(1)}, f32[4,4,128,128]{3,2,1,0:T(8,128)}, u32[]{:S(2)}) copy-start(f32[4,4,128,128]{3,2,1,0:T(8,128)} %param.6) | copy-start | bytes 3145732
  11.3 30.3 %copy-start.6 = (bf16[4,128,128]{2,1,0:T(8,128)(2,1)S(1)}, bf16[4,128,128]{2,1,0:T(8,128)(2,1)}, u32[]{:S(2)}) copy-start(bf16[4,128,128]{2,1,0:T(8,128)(2,1)} %constant.18.clone.tables_ref.refs_7_) | copy-start | bytes 393220
  11.3 30.3 %copy-start.8 = (f32[2,128,128]{2,1,0:T(8,128)S(1)}, f32[2,128,128]{2,1,0:T(8,128)}, u32[]{:S(2)}) copy-start(f32[2,128,128]{2,1,0:T(8,128)} %constant.19.clone.refs_6_) | copy-start | bytes 393220
  11.5 17.3 %collective-permute-start.2 = (f32[2,200,64]{2,1,0:T(8,128)S(1)}, f32[2,200,64]{2,1,0:T(8,128)S(1)}, u32[]{:S(2)}, u32[]{:S(2)}) collective-permute-start(f32[2,200,64]{2,1,0:T(8,128)S(1)} %get-tuple-element.28), channel_id=1, source_target_pairs={{0,1},{1,2},{2,3},{3,4},{4,5},{5,6},{6,7},{7,8},{8,9},{9,10},{10,1... | collective-permute-start | bytes 307208 | tf_op jit(solution)/shard_map/ppermute | solution.py:392
  11.6 17.2 %collective-permute-start.3 = (f32[2,200,64]{2,1,0:T(8,128)S(1)}, f32[2,200,64]{2,1,0:T(8,128)S(1)}, u32[]{:S(2)}, u32[]{:S(2)}) collective-permute-start(f32[2,200,64]{2,1,0:T(8,128)S(1)} %get-tuple-element.29), channel_id=1, source_target_pairs={{0,15},{1,0},{2,1},{3,2},{4,3},{5,4},{6,5},{7,6},{8,7},{9,8},{10,9... | collective-permute-start | bytes 307208 | tf_op jit(solution)/shard_map/ppermute | solution.py:393
  16.9 24.4 %all-to-all-start = ((f32[256,1,128]{2,1,0:T(1,128)}), f32[256,1,128]{2,1,0:T(1,128)S(1)}, u32[]{:S(2)}, u32[]{:S(2)}) async-start(f32[256,1,128]{2,1,0:T(1,128)} %bitcast.4), calls=%async_computation | async-start | bytes 262144 | tf_op jit(solution)/shard_map/all_to_all | solution.py:337
  29.8 11.9 %copy-start = (f32[4,200,128]{2,1,0:T(8,128)S(1)}, f32[4,200,128]{2,1,0:T(8,128)}, u32[]{:S(2)}) copy-start(f32[4,200,128]{2,1,0:T(8,128)} %maximum_maximum_fusion.ext_ref.refs_4_) | copy-start | bytes 1228804
  41.6 46.7 %copy-start.5 = (f32[2,72,72]{2,1,0:T(8,128)S(1)}, f32[2,72,72]{2,1,0:T(8,128)}, u32[]{:S(2)}) copy-start(f32[2,72,72]{2,1,0:T(8,128)} %refs_2_.1) | copy-start | bytes 124420
  51.9 14.0 %all-to-all-start.1 = ((f32[32,16,128]{2,1,0:T(8,128)}), f32[32,16,128]{2,1,0:T(8,128)S(1)}, u32[]{:S(2)}, u32[]{:S(2)}) async-start(f32[32,16,128]{2,1,0:T(8,128)} %bitcast.7), calls=%async_computation.1 | async-start | bytes 524288 | tf_op jit(solution)/shard_map/all_to_all | solution.py:337
  56.8 17.2 %collective-permute-start.5 = (f32[4,64,128]{2,1,0:T(8,128)S(1)}, f32[4,64,128]{2,1,0:T(8,128)S(1)}, u32[]{:S(2)}, u32[]{:S(2)}) collective-permute-start(f32[4,64,128]{2,1,0:T(8,128)S(1)} %get-tuple-element.26), channel_id=1, source_target_pairs={{0,16},{16,32},{32,48},{48,64},{64,80},{80,96},{96,112},{112,128},... | collective-permute-start | bytes 393224 | tf_op jit(solution)/shard_map/ppermute | solution.py:444
  60.3 13.8 %collective-permute-start.4 = (f32[4,64,128]{2,1,0:T(8,128)S(1)}, f32[4,64,128]{2,1,0:T(8,128)S(1)}, u32[]{:S(2)}, u32[]{:S(2)}) collective-permute-start(f32[4,64,128]{2,1,0:T(8,128)S(1)} %get-tuple-element.27), channel_id=1, source_target_pairs={{0,240},{16,0},{32,16},{48,32},{64,48},{80,64},{96,80},{112,96},{1... | collective-permute-start | bytes 393224 | tf_op jit(solution)/shard_map/ppermute | solution.py:443
  66.6 14.7 %all-to-all-start.2 = ((f32[8,16,128]{2,1,0:T(8,128)}), f32[8,16,128]{2,1,0:T(8,128)S(1)}, u32[]{:S(2)}, u32[]{:S(2)}) async-start(f32[8,16,128]{2,1,0:T(8,128)} %broadcast_in_dim.7), calls=%async_computation.2 | async-start | bytes 131072 | tf_op jit(solution)/shard_map/all_to_all | solution.py:337
  74.2 14.1 %collective-permute-start.7 = (f32[2,72,64]{2,1,0:T(8,128)S(1)}, f32[2,72,64]{2,1,0:T(8,128)S(1)}, u32[]{:S(2)}, u32[]{:S(2)}) collective-permute-start(f32[2,72,64]{2,1,0:T(8,128)S(1)} %get-tuple-element.30), channel_id=1, source_target_pairs={{0,1},{1,2},{2,3},{3,4},{4,5},{5,6},{6,7},{7,8},{8,9},{9,10},{10,1... | collective-permute-start | bytes 110600 | tf_op jit(solution)/shard_map/ppermute | solution.py:456
  74.3 14.0 %collective-permute-start.6 = (f32[2,72,64]{2,1,0:T(8,128)S(1)}, f32[2,72,64]{2,1,0:T(8,128)S(1)}, u32[]{:S(2)}, u32[]{:S(2)}) collective-permute-start(f32[2,72,64]{2,1,0:T(8,128)S(1)} %get-tuple-element.31), channel_id=1, source_target_pairs={{0,15},{1,0},{2,1},{3,2},{4,3},{5,4},{6,5},{7,6},{8,7},{9,8},{10,9... | collective-permute-start | bytes 110600 | tf_op jit(solution)/shard_map/ppermute | solution.py:455
  82.0 14.9 %all-to-all-start.3 = ((f32[32,16,128]{2,1,0:T(8,128)}), f32[32,16,128]{2,1,0:T(8,128)S(1)}, u32[]{:S(2)}, u32[]{:S(2)}) async-start(f32[32,16,128]{2,1,0:T(8,128)} %broadcast_in_dim.8), calls=%async_computation.3 | async-start | bytes 524288 | tf_op jit(solution)/shard_map/all_to_all | solution.py:337
